TPU v7x, 32 devices: a whole 2x2x4 slice. The times are simulated.
32 devices in a mesh: gx: 4 (over y, x), gy: 8 (over z, core).
Axes of the slice: x: 2, y: 2, z: 4, core: 2. Of those that a mesh axis runs over, the one named last changes fastest.
Arguments:
- velocity_u: float32 [16, 64, 1024], P(None, 'gx', 'gy'), may hold values from -4 to 4
- velocity_v: float32 [16, 64, 1024], P(None, 'gx', 'gy'), may hold values from -4 to 4
- buoyancy: float32 [16, 64, 1024], P(None, 'gx', 'gy'), may hold values from -5 to 5
- surface: float32 [64, 1024], P('gx', 'gy'), may hold values from -0.5 to 0.5
- transport_u: float32 [64, 1024], P('gx', 'gy'), may hold values from -2 to 2
- transport_v: float32 [64, 1024], P('gx', 'gy'), may hold values from -2 to 2
- ocean: int32 [64, 1024], P('gx', 'gy'), may hold values 0 or 1
- layers: int32 [64, 1024], P('gx', 'gy'), may hold values from 4 to 16
Outputs:
- new_u: float32 [16, 64, 1024], P(None, 'gx', 'gy')
- new_v: float32 [16, 64, 1024], P(None, 'gx', 'gy')
- new_buoyancy: float32 [16, 64, 1024], P(None, 'gx', 'gy')
- new_surface: float32 [64, 1024], P('gx', 'gy')
- new_transport_u: float32 [64, 1024], P('gx', 'gy')
- new_transport_v: float32 [64, 1024], P('gx', 'gy')
All inputs are finite; a program needn't handle non-finite values. No bound on the sum of `ocean` on one device may be relied on, other than what follows from the above.
Results may differ from a plain program's by a relative error of at most 0.0001.
Values sent between devices are 32-bit elements; how exact they have to be, the bound alone decides.
A program may use at most 64 MiB of HBM per device.

v0:
```python
import jax
import jax.numpy as jnp
from jax import lax
from jax.sharding import PartitionSpec as P

SUB = 8
STEPS = 2


PRESSURE_COEF = 0.5
CORIOLIS = 0.1
VISCOSITY = 0.02
TIME_STEP = 0.2
DIVERGENCE_COEF = 0.25
GRAVITY_COEF = 0.25
DRAG_KEEP = 0.98
SURFACE_CORIOLIS = 0.05


def padded(cells, sides, width):
    for axis, dim in sides:
        count = lax.axis_size(axis)
        ends = count - 1
        head = lax.slice_in_dim(cells, 0, width, axis=dim)
        tail = lax.slice_in_dim(cells, cells.shape[dim] - width, cells.shape[dim], axis=dim)
        cells = jnp.concatenate(
            [
                lax.ppermute(tail, axis, [(i, (i + 1) % count) for i in range(ends)]),
                cells,
                lax.ppermute(head, axis, [((i + 1) % count, i) for i in range(ends)]),
            ],
            axis=dim,
        )
    return cells


def trim_rim(field, width):
    return field[..., width : field.shape[-2] - width, width : field.shape[-1] - width]


def diff_x(field):
    return (field[..., 2:, 1:-1] - field[..., :-2, 1:-1]) * 0.5


def diff_y(field):
    return (field[..., 1:-1, 2:] - field[..., 1:-1, :-2]) * 0.5


def laplace(field):
    return (
        field[..., 2:, 1:-1]
        + field[..., :-2, 1:-1]
        + field[..., 1:-1, 2:]
        + field[..., 1:-1, :-2]
        - 4.0 * field[..., 1:-1, 1:-1]
    )


def advance(near_state, biharm, active):
    levels = near_state.shape[1]
    vel_u = trim_rim(near_state[0], 1)
    vel_v = trim_rim(near_state[1], 1)
    buoy_near = near_state[2]
    pressure = jnp.cumsum(buoy_near, axis=0) / levels
    tend_u = -PRESSURE_COEF * diff_x(pressure) + CORIOLIS * vel_v - VISCOSITY * biharm[0]
    tend_v = -PRESSURE_COEF * diff_y(pressure) - CORIOLIS * vel_u - VISCOSITY * biharm[1]
    tend_b = -(vel_u * diff_x(buoy_near) + vel_v * diff_y(buoy_near)) - VISCOSITY * biharm[2]
    star_u = active * (vel_u + TIME_STEP * tend_u)
    star_v = active * (vel_v + TIME_STEP * tend_v)
    new_buoy = active * (trim_rim(buoy_near, 1) + TIME_STEP * tend_b)
    force_u = jnp.sum(active * tend_u, axis=0) / levels
    force_v = jnp.sum(active * tend_v, axis=0) / levels
    return (star_u, star_v, new_buoy, force_u, force_v)


def surface_step(sea_level, flow_u, flow_v, force_u, force_v, wet_mask, column_depth):
    eta_mid = trim_rim(wet_mask, 1) * (
        trim_rim(sea_level, 1) - DIVERGENCE_COEF * (diff_x(flow_u) + diff_y(flow_v))
    )
    wet_inner = trim_rim(wet_mask, 2)
    total_depth = trim_rim(column_depth, 2) + trim_rim(eta_mid, 1)
    old_u = trim_rim(flow_u, 2)
    old_v = trim_rim(flow_v, 2)
    next_u = wet_inner * (
        DRAG_KEEP * old_u
        + TIME_STEP * trim_rim(force_u, 2)
        - GRAVITY_COEF * total_depth * diff_x(eta_mid)
        + SURFACE_CORIOLIS * old_v
    )
    next_v = wet_inner * (
        DRAG_KEEP * old_v
        + TIME_STEP * trim_rim(force_v, 2)
        - GRAVITY_COEF * total_depth * diff_y(eta_mid)
        - SURFACE_CORIOLIS * old_u
    )
    return (
        trim_rim(eta_mid, 1),
        next_u,
        next_v,
        trim_rim(force_u, 2),
        trim_rim(force_v, 2),
        wet_inner,
        trim_rim(column_depth, 2),
    )


def couple_columns(star_u, star_v, total_u, total_v, active, layer_count, column_depth, substeps):
    column_u = jnp.sum(star_u, axis=0) / layer_count
    column_v = jnp.sum(star_v, axis=0) / layer_count
    new_u = active * (star_u - column_u + total_u / substeps / column_depth)
    new_v = active * (star_v - column_v + total_v / substeps / column_depth)
    return (new_u, new_v)


def per_device(velocity_u, velocity_v, buoyancy, surface, transport_u, transport_v, ocean, layers):
    levels = velocity_u.shape[0]
    coast = padded(jnp.stack([ocean, layers]), (("gx", 1), ("gy", 2)), 8)
    wet_wide = coast[0].astype(jnp.float32)
    count_wide = coast[1]
    active_wide = wet_wide[None] * (jnp.arange(levels)[:, None, None] < count_wide[None]).astype(
        jnp.float32
    )
    depth_wide = count_wide.astype(jnp.float32) / levels
    active = trim_rim(active_wide, 8)
    layer_count = trim_rim(count_wide, 8).astype(jnp.float32)
    column_depth = trim_rim(depth_wide, 8)
    stacked = jnp.stack([velocity_u, velocity_v, buoyancy])
    sea_level, flow_u, flow_v = (surface, transport_u, transport_v)
    for step_index in range(STEPS):
        near_state = padded(stacked, (("gx", 2), ("gy", 3)), 1)
        lap_masked = active * laplace(near_state)
        biharm = laplace(padded(lap_masked, (("gx", 2), ("gy", 3)), 1))
        star_u, star_v, new_buoy, force_u, force_v = advance(near_state, biharm, active)
        total_u = jnp.zeros(surface.shape, jnp.float32)
        total_v = jnp.zeros(surface.shape, jnp.float32)
        for group_index in range(SUB // 4):
            bordered = padded(
                jnp.stack([sea_level, flow_u, flow_v, force_u, force_v]), (("gx", 1), ("gy", 2)), 8
            )
            pieces = (
                bordered[0],
                bordered[1],
                bordered[2],
                bordered[3],
                bordered[4],
                wet_wide,
                depth_wide,
            )
            for inner_index in range(4):
                pieces = surface_step(*pieces)
                margin = 6 - 2 * inner_index
                total_u = total_u + trim_rim(pieces[1], margin)
                total_v = total_v + trim_rim(pieces[2], margin)
            sea_level, flow_u, flow_v = (pieces[0], pieces[1], pieces[2])
        new_u, new_v = couple_columns(
            star_u, star_v, total_u, total_v, active, layer_count, column_depth, SUB
        )
        stacked = jnp.stack([new_u, new_v, new_buoy])
    return (stacked[0], stacked[1], stacked[2], sea_level, flow_u, flow_v)


def solution(mesh):
    return jax.shard_map(
        per_device,
        mesh=mesh,
        in_specs=(
            P(None, "gx", "gy"),
            P(None, "gx", "gy"),
            P(None, "gx", "gy"),
            P("gx", "gy"),
            P("gx", "gy"),
            P("gx", "gy"),
            P("gx", "gy"),
            P("gx", "gy"),
        ),
        out_specs=(
            P(None, "gx", "gy"),
            P(None, "gx", "gy"),
            P(None, "gx", "gy"),
            P("gx", "gy"),
            P("gx", "gy"),
            P("gx", "gy"),
        ),
        check_vma=False,
    )
```

profile of v0, /device:TPU:1, one launch (start us, length us, event | category | flops | bytes accessed | tf_op | source)
XLA Modules:
  0.0 176.5 jit_solution(1479442177628310359)
XLA Ops:
  0.7 0.8 fusion.287
  1.5 3.9 %collective-permute-start = (s32[2,8,128]{2,1,0:T(8,128)S(1)}, s32[2,8,128]{2,1,0:T(8,128)S(1)}, u32[]{:S(2)}, u32[]{:S(2)}) collective-permute-start(s32[2,8,128]{2,1,0:T(8,128)S(1)} %get-tuple-element.135), channel_id=1, source_target_pairs={{0,8},{8,16},{16,24},{1,9},{9,17},{17,25},{2,10},{10,18},{18,26},{... | collective-permute-start | bytes 24584 | tf_op jit(solution)/shard_map/ppermute | solution.py:28
  5.4 1.3 collective-permute-start.1
  6.7 1.1 pad_maximum_fusion.54
  7.8 4.0 %collective-permute-start.4 = (f32[3,16,1,128]{3,2,1,0:T(1,128)S(1)}, f32[3,16,1,128]{3,2,1,0:T(1,128)S(1)}, u32[]{:S(2)}, u32[]{:S(2)}) collective-permute-start(f32[3,16,1,128]{3,2,1,0:T(1,128)S(1)} %get-tuple-element.61), channel_id=1, source_target_pairs={{0,8},{8,16},{16,24},{1,9},{9,17},{17,25},{2,10},{10,18},{18,26},{... | collective-permute-start | bytes 73736 | tf_op jit(solution)/shard_map/ppermute | solution.py:28
  11.8 1.3 collective-permute-start.5
  13.1 0.7 constant_dynamic-update-slice_fusion.4
  13.8 0.7 constant_dynamic-update-slice_fusion.3
  14.5 0.7 pad_add_fusion.1
  15.3 4.6 %collective-permute-start.2 = (s32[2,32,8]{2,1,0:T(8,128)S(1)}, s32[2,32,8]{2,1,0:T(8,128)S(1)}, u32[]{:S(2)}, u32[]{:S(2)}) collective-permute-start(s32[2,32,8]{2,1,0:T(8,128)S(1)} %get-tuple-element.129), channel_id=1, source_target_pairs={{0,1},{1,2},{2,3},{3,4},{4,5},{5,6},{6,7},{8,9},{9,10},{10,11},{11... | collective-permute-start | bytes 6152 | tf_op jit(solution)/shard_map/ppermute | solution.py:28
  19.9 1.9 %collective-permute-start.3 = (s32[2,32,8]{2,1,0:T(8,128)S(1)}, s32[2,32,8]{2,1,0:T(8,128)S(1)}, u32[]{:S(2)}, u32[]{:S(2)}) collective-permute-start(s32[2,32,8]{2,1,0:T(8,128)S(1)} %get-tuple-element.130), channel_id=1, source_target_pairs={{1,0},{2,1},{3,2},{4,3},{5,4},{6,5},{7,6},{9,8},{10,9},{11,10},{12... | collective-permute-start | bytes 6152 | tf_op jit(solution)/shard_map/ppermute | solution.py:30
  21.9 0.7 constant_dynamic-update-slice_fusion.2
  22.6 2.6 %collective-permute-done.3 = s32[2,32,8]{2,1,0:T(8,128)S(1)} collective-permute-done((s32[2,32,8]{2,1,0:T(8,128)S(1)}, s32[2,32,8]{2,1,0:T(8,128)S(1)}, u32[]{:S(2)}, u32[]{:S(2)}) %collective-permute-start.3) | collective-permute-done | bytes 2080 | tf_op jit(solution)/shard_map/ppermute | solution.py:30
  26.3 1.9 %collective-permute-start.6 = (f32[3,16,18,1]{2,1,3,0:T(8,128)S(1)}, f32[3,16,18,1]{2,1,3,0:T(8,128)S(1)}, u32[]{:S(2)}, u32[]{:S(2)}) collective-permute-start(f32[3,16,18,1]{2,1,3,0:T(8,128)S(1)} %copy.14), channel_id=1, source_target_pairs={{0,1},{1,2},{2,3},{3,4},{4,5},{5,6},{6,7},{8,9},{9,10},{10,11},{11... | collective-permute-start | bytes 10376 | tf_op jit(solution)/shard_map/ppermute | solution.py:28
  28.6 2.4 %collective-permute-start.7 = (f32[3,16,18,1]{2,1,3,0:T(8,128)S(1)}, f32[3,16,18,1]{2,1,3,0:T(8,128)S(1)}, u32[]{:S(2)}, u32[]{:S(2)}) collective-permute-start(f32[3,16,18,1]{2,1,3,0:T(8,128)S(1)} %copy.15), channel_id=1, source_target_pairs={{1,0},{2,1},{3,2},{4,3},{5,4},{6,5},{7,6},{9,8},{10,9},{11,10},{12... | collective-permute-start | bytes 10376 | tf_op jit(solution)/shard_map/ppermute | solution.py:30
  31.5 2.3 %collective-permute-done.7 = f32[3,16,18,1]{2,1,3,0:T(8,128)S(1)} collective-permute-done((f32[3,16,18,1]{2,1,3,0:T(8,128)S(1)}, f32[3,16,18,1]{2,1,3,0:T(8,128)S(1)}, u32[]{:S(2)}, u32[]{:S(2)}) %collective-permute-start.7) | collective-permute-done | bytes 3488 | tf_op jit(solution)/shard_map/ppermute | solution.py:30
  34.7 1.3 collective-permute-start.8
  36.0 5.3 %collective-permute-start.9 = (f32[3,16,1,128]{3,2,1,0:T(1,128)S(1)}, f32[3,16,1,128]{3,2,1,0:T(1,128)S(1)}, u32[]{:S(2)}, u32[]{:S(2)}) collective-permute-start(f32[3,16,1,128]{3,2,1,0:T(1,128)S(1)} %get-tuple-element.59), channel_id=1, source_target_pairs={{0,8},{8,16},{16,24},{1,9},{9,17},{17,25},{2,10},{10,18},{18,26},{... | collective-permute-start | bytes 73736 | tf_op jit(solution)/shard_map/ppermute | solution.py:28
  41.3 0.7 pad_maximum_fusion
  42.0 1.0 slice_bitcast_fusion.4
  45.0 1.9 %collective-permute-start.10 = (f32[3,16,18,1]{2,1,3,0:T(8,128)S(1)}, f32[3,16,18,1]{2,1,3,0:T(8,128)S(1)}, u32[]{:S(2)}, u32[]{:S(2)}) collective-permute-start(f32[3,16,18,1]{2,1,3,0:T(8,128)S(1)} %copy.20), channel_id=1, source_target_pairs={{1,0},{2,1},{3,2},{4,3},{5,4},{6,5},{7,6},{9,8},{10,9},{11,10},{12... | collective-permute-start | bytes 10376 | tf_op jit(solution)/shard_map/ppermute | solution.py:30
  47.3 3.6 %collective-permute-start.11 = (f32[3,16,18,1]{2,1,3,0:T(8,128)S(1)}, f32[3,16,18,1]{2,1,3,0:T(8,128)S(1)}, u32[]{:S(2)}, u32[]{:S(2)}) collective-permute-start(f32[3,16,18,1]{2,1,3,0:T(8,128)S(1)} %copy.22), channel_id=1, source_target_pairs={{0,1},{1,2},{2,3},{3,4},{4,5},{5,6},{6,7},{8,9},{9,10},{10,11},{11... | collective-permute-start | bytes 10376 | tf_op jit(solution)/shard_map/ppermute | solution.py:28
  52.8 1.5 fusion.283
  54.4 4.5 %collective-permute-start.12 = (f32[5,8,128]{2,1,0:T(8,128)S(1)}, f32[5,8,128]{2,1,0:T(8,128)S(1)}, u32[]{:S(2)}, u32[]{:S(2)}) collective-permute-start(f32[5,8,128]{2,1,0:T(8,128)S(1)} %get-tuple-element.123), channel_id=1, source_target_pairs={{0,8},{8,16},{16,24},{1,9},{9,17},{17,25},{2,10},{10,18},{18,26},{... | collective-permute-start | bytes 61448 | tf_op jit(solution)/shard_map/ppermute | solution.py:28
  58.9 1.3 collective-permute-start.13
  60.3 3.2 %collective-permute-done.13 = f32[5,8,128]{2,1,0:T(8,128)S(1)} collective-permute-done((f32[5,8,128]{2,1,0:T(8,128)S(1)}, f32[5,8,128]{2,1,0:T(8,128)S(1)}, u32[]{:S(2)}, u32[]{:S(2)}) %collective-permute-start.13) | collective-permute-done | bytes 20512 | tf_op jit(solution)/shard_map/ppermute | solution.py:30
  63.6 5.6 %collective-permute-start.14 = (f32[5,32,8]{2,1,0:T(8,128)S(1)}, f32[5,32,8]{2,1,0:T(8,128)S(1)}, u32[]{:S(2)}, u32[]{:S(2)}) collective-permute-start(f32[5,32,8]{2,1,0:T(8,128)S(1)} %get-tuple-element.113), channel_id=1, source_target_pairs={{0,1},{1,2},{2,3},{3,4},{4,5},{5,6},{6,7},{8,9},{9,10},{10,11},{11... | collective-permute-start | bytes 15368 | tf_op jit(solution)/shard_map/ppermute | solution.py:28
  69.2 1.9 %collective-permute-start.15 = (f32[5,32,8]{2,1,0:T(8,128)S(1)}, f32[5,32,8]{2,1,0:T(8,128)S(1)}, u32[]{:S(2)}, u32[]{:S(2)}) collective-permute-start(f32[5,32,8]{2,1,0:T(8,128)S(1)} %get-tuple-element.114), channel_id=1, source_target_pairs={{1,0},{2,1},{3,2},{4,3},{5,4},{6,5},{7,6},{9,8},{10,9},{11,10},{12... | collective-permute-start | bytes 15368 | tf_op jit(solution)/shard_map/ppermute | solution.py:30
  71.2 3.8 %collective-permute-done.15 = f32[5,32,8]{2,1,0:T(8,128)S(1)} collective-permute-done((f32[5,32,8]{2,1,0:T(8,128)S(1)}, f32[5,32,8]{2,1,0:T(8,128)S(1)}, u32[]{:S(2)}, u32[]{:S(2)}) %collective-permute-start.15) | collective-permute-done | bytes 5152 | tf_op jit(solution)/shard_map/ppermute | solution.py:30
  76.3 4.3 %collective-permute-start.16 = (f32[5,8,128]{2,1,0:T(8,128)S(1)}, f32[5,8,128]{2,1,0:T(8,128)S(1)}, u32[]{:S(2)}, u32[]{:S(2)}) collective-permute-start(f32[5,8,128]{2,1,0:T(8,128)S(1)} %get-tuple-element.121), channel_id=1, source_target_pairs={{0,8},{8,16},{16,24},{1,9},{9,17},{17,25},{2,10},{10,18},{18,26},{... | collective-permute-start | bytes 61448 | tf_op jit(solution)/shard_map/ppermute | solution.py:28
  80.6 1.3 collective-permute-start.17
  81.9 3.2 %collective-permute-done.17 = f32[5,8,128]{2,1,0:T(8,128)S(1)} collective-permute-done((f32[5,8,128]{2,1,0:T(8,128)S(1)}, f32[5,8,128]{2,1,0:T(8,128)S(1)}, u32[]{:S(2)}, u32[]{:S(2)}) %collective-permute-start.17) | collective-permute-done | bytes 20512 | tf_op jit(solution)/shard_map/ppermute | solution.py:30
  85.2 3.3 %collective-permute-start.18 = (f32[5,32,8]{2,1,0:T(8,128)S(1)}, f32[5,32,8]{2,1,0:T(8,128)S(1)}, u32[]{:S(2)}, u32[]{:S(2)}) collective-permute-start(f32[5,32,8]{2,1,0:T(8,128)S(1)} %get-tuple-element.111), channel_id=1, source_target_pairs={{0,1},{1,2},{2,3},{3,4},{4,5},{5,6},{6,7},{8,9},{9,10},{10,11},{11... | collective-permute-start | bytes 15368 | tf_op jit(solution)/shard_map/ppermute | solution.py:28
  88.5 1.9 %collective-permute-start.19 = (f32[5,32,8]{2,1,0:T(8,128)S(1)}, f32[5,32,8]{2,1,0:T(8,128)S(1)}, u32[]{:S(2)}, u32[]{:S(2)}) collective-permute-start(f32[5,32,8]{2,1,0:T(8,128)S(1)} %get-tuple-element.112), channel_id=1, source_target_pairs={{1,0},{2,1},{3,2},{4,3},{5,4},{6,5},{7,6},{9,8},{10,9},{11,10},{12... | collective-permute-start | bytes 15368 | tf_op jit(solution)/shard_map/ppermute | solution.py:30
  90.4 0.8 convert_divide_fusion.3
  91.2 3.0 %collective-permute-done.19 = f32[5,32,8]{2,1,0:T(8,128)S(1)} collective-permute-done((f32[5,32,8]{2,1,0:T(8,128)S(1)}, f32[5,32,8]{2,1,0:T(8,128)S(1)}, u32[]{:S(2)}, u32[]{:S(2)}) %collective-permute-start.19) | collective-permute-done | bytes 5152 | tf_op jit(solution)/shard_map/ppermute | solution.py:30
  95.6 1.3 fusion.20
  97.0 2.5 %collective-permute-start.20 = (f32[3,16,1,128]{3,2,1,0:T(1,128)S(1)}, f32[3,16,1,128]{3,2,1,0:T(1,128)S(1)}, u32[]{:S(2)}, u32[]{:S(2)}) collective-permute-start(f32[3,16,1,128]{3,2,1,0:T(1,128)S(1)} %get-tuple-element.57), channel_id=1, source_target_pairs={{0,8},{8,16},{16,24},{1,9},{9,17},{17,25},{2,10},{10,18},{18,26},{... | collective-permute-start | bytes 73736 | tf_op jit(solution)/shard_map/ppermute | solution.py:28
  99.5 1.3 collective-permute-start.21
  100.8 3.2 %collective-permute-done.21 = f32[3,16,1,128]{3,2,1,0:T(1,128)S(1)} collective-permute-done((f32[3,16,1,128]{3,2,1,0:T(1,128)S(1)}, f32[3,16,1,128]{3,2,1,0:T(1,128)S(1)}, u32[]{:S(2)}, u32[]{:S(2)}) %collective-permute-start.21) | collective-permute-done | bytes 24608 | tf_op jit(solution)/shard_map/ppermute | solution.py:30
  104.8 3.3 %collective-permute-start.22 = (f32[3,16,18,1]{2,1,3,0:T(8,128)S(1)}, f32[3,16,18,1]{2,1,3,0:T(8,128)S(1)}, u32[]{:S(2)}, u32[]{:S(2)}) collective-permute-start(f32[3,16,18,1]{2,1,3,0:T(8,128)S(1)} %copy.24), channel_id=1, source_target_pairs={{0,1},{1,2},{2,3},{3,4},{4,5},{5,6},{6,7},{8,9},{9,10},{10,11},{11... | collective-permute-start | bytes 10376 | tf_op jit(solution)/shard_map/ppermute | solution.py:28
  108.4 1.9 %collective-permute-start.23 = (f32[3,16,18,1]{2,1,3,0:T(8,128)S(1)}, f32[3,16,18,1]{2,1,3,0:T(8,128)S(1)}, u32[]{:S(2)}, u32[]{:S(2)}) collective-permute-start(f32[3,16,18,1]{2,1,3,0:T(8,128)S(1)} %copy.25), channel_id=1, source_target_pairs={{1,0},{2,1},{3,2},{4,3},{5,4},{6,5},{7,6},{9,8},{10,9},{11,10},{12... | collective-permute-start | bytes 10376 | tf_op jit(solution)/shard_map/ppermute | solution.py:30
  110.8 2.8 %collective-permute-done.23 = f32[3,16,18,1]{2,1,3,0:T(8,128)S(1)} collective-permute-done((f32[3,16,18,1]{2,1,3,0:T(8,128)S(1)}, f32[3,16,18,1]{2,1,3,0:T(8,128)S(1)}, u32[]{:S(2)}, u32[]{:S(2)}) %collective-permute-start.23) | collective-permute-done | bytes 3488 | tf_op jit(solution)/shard_map/ppermute | solution.py:30
  114.6 1.3 collective-permute-start.24
  115.9 4.0 %collective-permute-start.25 = (f32[3,16,1,128]{3,2,1,0:T(1,128)S(1)}, f32[3,16,1,128]{3,2,1,0:T(1,128)S(1)}, u32[]{:S(2)}, u32[]{:S(2)}) collective-permute-start(f32[3,16,1,128]{3,2,1,0:T(1,128)S(1)} %get-tuple-element.55), channel_id=1, source_target_pairs={{0,8},{8,16},{16,24},{1,9},{9,17},{17,25},{2,10},{10,18},{18,26},{... | collective-permute-start | bytes 73736 | tf_op jit(solution)/shard_map/ppermute | solution.py:28
  119.8 0.7 pad_maximum_fusion.1
  120.6 1.0 slice_bitcast_fusion.1
  122.3 1.9 %collective-permute-start.26 = (f32[3,16,18,1]{2,1,3,0:T(8,128)S(1)}, f32[3,16,18,1]{2,1,3,0:T(8,128)S(1)}, u32[]{:S(2)}, u32[]{:S(2)}) collective-permute-start(f32[3,16,18,1]{2,1,3,0:T(8,128)S(1)} %copy.30), channel_id=1, source_target_pairs={{1,0},{2,1},{3,2},{4,3},{5,4},{6,5},{7,6},{9,8},{10,9},{11,10},{12... | collective-permute-start | bytes 10376 | tf_op jit(solution)/shard_map/ppermute | solution.py:30
  124.6 3.8 %collective-permute-start.27 = (f32[3,16,18,1]{2,1,3,0:T(8,128)S(1)}, f32[3,16,18,1]{2,1,3,0:T(8,128)S(1)}, u32[]{:S(2)}, u32[]{:S(2)}) collective-permute-start(f32[3,16,18,1]{2,1,3,0:T(8,128)S(1)} %copy.32), channel_id=1, source_target_pairs={{0,1},{1,2},{2,3},{3,4},{4,5},{5,6},{6,7},{8,9},{9,10},{10,11},{11... | collective-permute-start | bytes 10376 | tf_op jit(solution)/shard_map/ppermute | solution.py:28
  130.1 2.2 %fusion.286 = (f32[16,128]{1,0:T(8,128)S(1)}, f32[16,128]{1,0:T(8,128)S(1)}, f32[16,128]{1,0:T(8,128)S(1)}, f32[16,128]{1,0:T(8,128)S(1)}, f32[16,16,128]{2,1,0:...) fusion(f32[16,18,130]{2,1,0:T(8,128)} %get-tuple-element.42, f32[16,128]{1,0:T(8,128)S(1)} %slice.1613, ...), kind=kLoop, calls=%fused_computation.524 | loop fusion | flops 1269760 | bytes 2277376 | tf_op jit(solution)/shard_map/reduce_sum | solution.py:109
  132.3 3.4 %collective-permute-start.28 = (f32[5,8,128]{2,1,0:T(8,128)S(1)}, f32[5,8,128]{2,1,0:T(8,128)S(1)}, u32[]{:S(2)}, u32[]{:S(2)}) collective-permute-start(f32[5,8,128]{2,1,0:T(8,128)S(1)} %get-tuple-element.119), channel_id=1, source_target_pairs={{0,8},{8,16},{16,24},{1,9},{9,17},{17,25},{2,10},{10,18},{18,26},{... | collective-permute-start | bytes 61448 | tf_op jit(solution)/shard_map/ppermute | solution.py:28
  135.7 1.3 collective-permute-start.29
  137.0 3.6 %collective-permute-done.29 = f32[5,8,128]{2,1,0:T(8,128)S(1)} collective-permute-done((f32[5,8,128]{2,1,0:T(8,128)S(1)}, f32[5,8,128]{2,1,0:T(8,128)S(1)}, u32[]{:S(2)}, u32[]{:S(2)}) %collective-permute-start.29) | collective-permute-done | bytes 20512 | tf_op jit(solution)/shard_map/ppermute | solution.py:30
  140.7 5.4 %collective-permute-start.30 = (f32[5,32,8]{2,1,0:T(8,128)S(1)}, f32[5,32,8]{2,1,0:T(8,128)S(1)}, u32[]{:S(2)}, u32[]{:S(2)}) collective-permute-start(f32[5,32,8]{2,1,0:T(8,128)S(1)} %get-tuple-element.109), channel_id=1, source_target_pairs={{0,1},{1,2},{2,3},{3,4},{4,5},{5,6},{6,7},{8,9},{9,10},{10,11},{11... | collective-permute-start | bytes 15368 | tf_op jit(solution)/shard_map/ppermute | solution.py:28
  146.1 1.9 %collective-permute-start.31 = (f32[5,32,8]{2,1,0:T(8,128)S(1)}, f32[5,32,8]{2,1,0:T(8,128)S(1)}, u32[]{:S(2)}, u32[]{:S(2)}) collective-permute-start(f32[5,32,8]{2,1,0:T(8,128)S(1)} %get-tuple-element.110), channel_id=1, source_target_pairs={{1,0},{2,1},{3,2},{4,3},{5,4},{6,5},{7,6},{9,8},{10,9},{11,10},{12... | collective-permute-start | bytes 15368 | tf_op jit(solution)/shard_map/ppermute | solution.py:30
  148.0 3.8 %collective-permute-done.31 = f32[5,32,8]{2,1,0:T(8,128)S(1)} collective-permute-done((f32[5,32,8]{2,1,0:T(8,128)S(1)}, f32[5,32,8]{2,1,0:T(8,128)S(1)}, u32[]{:S(2)}, u32[]{:S(2)}) %collective-permute-start.31) | collective-permute-done | bytes 5152 | tf_op jit(solution)/shard_map/ppermute | solution.py:30
  153.2 4.5 %collective-permute-start.32 = (f32[5,8,128]{2,1,0:T(8,128)S(1)}, f32[5,8,128]{2,1,0:T(8,128)S(1)}, u32[]{:S(2)}, u32[]{:S(2)}) collective-permute-start(f32[5,8,128]{2,1,0:T(8,128)S(1)} %get-tuple-element.117), channel_id=1, source_target_pairs={{0,8},{8,16},{16,24},{1,9},{9,17},{17,25},{2,10},{10,18},{18,26},{... | collective-permute-start | bytes 61448 | tf_op jit(solution)/shard_map/ppermute | solution.py:28
  157.7 1.3 collective-permute-start.33
  159.0 3.2 %collective-permute-done.33 = f32[5,8,128]{2,1,0:T(8,128)S(1)} collective-permute-done((f32[5,8,128]{2,1,0:T(8,128)S(1)}, f32[5,8,128]{2,1,0:T(8,128)S(1)}, u32[]{:S(2)}, u32[]{:S(2)}) %collective-permute-start.33) | collective-permute-done | bytes 20512 | tf_op jit(solution)/shard_map/ppermute | solution.py:30
  162.3 3.3 %collective-permute-start.34 = (f32[5,32,8]{2,1,0:T(8,128)S(1)}, f32[5,32,8]{2,1,0:T(8,128)S(1)}, u32[]{:S(2)}, u32[]{:S(2)}) collective-permute-start(f32[5,32,8]{2,1,0:T(8,128)S(1)} %get-tuple-element.107), channel_id=1, source_target_pairs={{0,1},{1,2},{2,3},{3,4},{4,5},{5,6},{6,7},{8,9},{9,10},{10,11},{11... | collective-permute-start | bytes 15368 | tf_op jit(solution)/shard_map/ppermute | solution.py:28
  165.6 1.9 %collective-permute-start.35 = (f32[5,32,8]{2,1,0:T(8,128)S(1)}, f32[5,32,8]{2,1,0:T(8,128)S(1)}, u32[]{:S(2)}, u32[]{:S(2)}) collective-permute-start(f32[5,32,8]{2,1,0:T(8,128)S(1)} %get-tuple-element.108), channel_id=1, source_target_pairs={{1,0},{2,1},{3,2},{4,3},{5,4},{6,5},{7,6},{9,8},{10,9},{11,10},{12... | collective-permute-start | bytes 15368 | tf_op jit(solution)/shard_map/ppermute | solution.py:30
  167.6 3.8 %collective-permute-done.35 = f32[5,32,8]{2,1,0:T(8,128)S(1)} collective-permute-done((f32[5,32,8]{2,1,0:T(8,128)S(1)}, f32[5,32,8]{2,1,0:T(8,128)S(1)}, u32[]{:S(2)}, u32[]{:S(2)}) %collective-permute-start.35) | collective-permute-done | bytes 5152 | tf_op jit(solution)/shard_map/ppermute | solution.py:30
  172.4 1.4 fusion.297
  174.6 2.0 %select_multiply_fusion = (f32[16,16,128]{2,1,0:T(8,128)}, f32[16,16,128]{2,1,0:T(8,128)}) fusion(f32[16,128]{1,0:T(8,128)S(1)} %slice.1613, s32[16,128]{1,0:T(8,128)S(1)} %copy-done.7, f32[16,128]{1,0:T(8,128)S(1)} %get-tuple-element.18, f32[16,128]{1,0:T(8,128)S(1)} %get-tuple-element.138, f32[16,16,128]{2,1,0:T(8,128)S(1)} %get-tuple-element.28, ...), kind=kLoop, calls=%fused_computation.8 | loop fusion | flops 458752 | bytes 835584 | tf_op jit(solution)/shard_map/mul | solution.py:111
  (166 shorter events, 18.2 us)
Async XLA Ops:
  0.6 24.5 %copy-start.13 = (s32[16,128]{1,0:T(8,128)S(1)}, s32[16,128]{1,0:T(8,128)}, u32[]{:S(2)}) copy-start(s32[16,128]{1,0:T(8,128)} %param.14) | copy-start | bytes 24580
  0.6 24.5 %copy-start.14 = (s32[16,128]{1,0:T(8,128)S(1)}, s32[16,128]{1,0:T(8,128)}, u32[]{:S(2)}) copy-start(s32[16,128]{1,0:T(8,128)} %param.15) | copy-start | bytes 24580
  0.7 24.8 %copy-start.2 = (f32[16,16,128]{2,1,0:T(8,128)S(1)}, f32[16,16,128]{2,1,0:T(8,128)}, u32[]{:S(2)}) copy-start(f32[16,16,128]{2,1,0:T(8,128)} %param.8) | copy-start | bytes 393220
  0.7 24.8 %copy-start.1 = (f32[16,16,128]{2,1,0:T(8,128)S(1)}, f32[16,16,128]{2,1,0:T(8,128)}, u32[]{:S(2)}) copy-start(f32[16,16,128]{2,1,0:T(8,128)} %param.9) | copy-start | bytes 393220
  0.7 24.8 %copy-start = (f32[16,16,128]{2,1,0:T(8,128)S(1)}, f32[16,16,128]{2,1,0:T(8,128)}, u32[]{:S(2)}) copy-start(f32[16,16,128]{2,1,0:T(8,128)} %param.10) | copy-start | bytes 393220
  1.5 13.0 %collective-permute-start = (s32[2,8,128]{2,1,0:T(8,128)S(1)}, s32[2,8,128]{2,1,0:T(8,128)S(1)}, u32[]{:S(2)}, u32[]{:S(2)}) collective-permute-start(s32[2,8,128]{2,1,0:T(8,128)S(1)} %get-tuple-element.135), channel_id=1, source_target_pairs={{0,8},{8,16},{16,24},{1,9},{9,17},{17,25},{2,10},{10,18},{18,26},{... | collective-permute-start | bytes 24584 | tf_op jit(solution)/shard_map/ppermute | solution.py:28
  5.4 9.1 %collective-permute-start.1 = (s32[2,8,128]{2,1,0:T(8,128)S(1)}, s32[2,8,128]{2,1,0:T(8,128)S(1)}, u32[]{:S(2)}, u32[]{:S(2)}) collective-permute-start(s32[2,8,128]{2,1,0:T(8,128)S(1)} %get-tuple-element.136), channel_id=1, source_target_pairs={{8,0},{16,8},{24,16},{9,1},{17,9},{25,17},{10,2},{18,10},{26,18},{... | collective-permute-start | bytes 24584 | tf_op jit(solution)/shard_map/ppermute | solution.py:30
  7.8 17.6 %collective-permute-start.4 = (f32[3,16,1,128]{3,2,1,0:T(1,128)S(1)}, f32[3,16,1,128]{3,2,1,0:T(1,128)S(1)}, u32[]{:S(2)}, u32[]{:S(2)}) collective-permute-start(f32[3,16,1,128]{3,2,1,0:T(1,128)S(1)} %get-tuple-element.61), channel_id=1, source_target_pairs={{0,8},{8,16},{16,24},{1,9},{9,17},{17,25},{2,10},{10,18},{18,26},{... | collective-permute-start | bytes 73736 | tf_op jit(solution)/shard_map/ppermute | solution.py:28
  11.8 13.6 %collective-permute-start.5 = (f32[3,16,1,128]{3,2,1,0:T(1,128)S(1)}, f32[3,16,1,128]{3,2,1,0:T(1,128)S(1)}, u32[]{:S(2)}, u32[]{:S(2)}) collective-permute-start(f32[3,16,1,128]{3,2,1,0:T(1,128)S(1)} %get-tuple-element.62), channel_id=1, source_target_pairs={{8,0},{16,8},{24,16},{9,1},{17,9},{25,17},{10,2},{18,10},{26,18},{... | collective-permute-start | bytes 73736 | tf_op jit(solution)/shard_map/ppermute | solution.py:30
  15.3 7.2 %collective-permute-start.2 = (s32[2,32,8]{2,1,0:T(8,128)S(1)}, s32[2,32,8]{2,1,0:T(8,128)S(1)}, u32[]{:S(2)}, u32[]{:S(2)}) collective-permute-start(s32[2,32,8]{2,1,0:T(8,128)S(1)} %get-tuple-element.129), channel_id=1, source_target_pairs={{0,1},{1,2},{2,3},{3,4},{4,5},{5,6},{6,7},{8,9},{9,10},{10,11},{11... | collective-permute-start | bytes 6152 | tf_op jit(solution)/shard_map/ppermute | solution.py:28
  19.9 5.2 %collective-permute-start.3 = (s32[2,32,8]{2,1,0:T(8,128)S(1)}, s32[2,32,8]{2,1,0:T(8,128)S(1)}, u32[]{:S(2)}, u32[]{:S(2)}) collective-permute-start(s32[2,32,8]{2,1,0:T(8,128)S(1)} %get-tuple-element.130), channel_id=1, source_target_pairs={{1,0},{2,1},{3,2},{4,3},{5,4},{6,5},{7,6},{9,8},{10,9},{11,10},{12... | collective-permute-start | bytes 6152 | tf_op jit(solution)/shard_map/ppermute | solution.py:30
  25.3 0.6 copy-start.3
  25.3 0.6 copy-start.8
  25.5 5.6 %copy-start.5 = (s32[16,128]{1,0:T(8,128)}, s32[16,128]{1,0:T(8,128)S(1)}, u32[]{:S(2)}) copy-start(s32[16,128]{1,0:T(8,128)S(1)} %slice.1612) | copy-start | bytes 24580
  26.3 4.7 %collective-permute-start.6 = (f32[3,16,18,1]{2,1,3,0:T(8,128)S(1)}, f32[3,16,18,1]{2,1,3,0:T(8,128)S(1)}, u32[]{:S(2)}, u32[]{:S(2)}) collective-permute-start(f32[3,16,18,1]{2,1,3,0:T(8,128)S(1)} %copy.14), channel_id=1, source_target_pairs={{0,1},{1,2},{2,3},{3,4},{4,5},{5,6},{6,7},{8,9},{9,10},{10,11},{11... | collective-permute-start | bytes 10376 | tf_op jit(solution)/shard_map/ppermute | solution.py:28
  28.6 5.1 %collective-permute-start.7 = (f32[3,16,18,1]{2,1,3,0:T(8,128)S(1)}, f32[3,16,18,1]{2,1,3,0:T(8,128)S(1)}, u32[]{:S(2)}, u32[]{:S(2)}) collective-permute-start(f32[3,16,18,1]{2,1,3,0:T(8,128)S(1)} %copy.15), channel_id=1, source_target_pairs={{1,0},{2,1},{3,2},{4,3},{5,4},{6,5},{7,6},{9,8},{10,9},{11,10},{12... | collective-permute-start | bytes 10376 | tf_op jit(solution)/shard_map/ppermute | solution.py:30
  34.7 8.3 %collective-permute-start.8 = (f32[3,16,1,128]{3,2,1,0:T(1,128)S(1)}, f32[3,16,1,128]{3,2,1,0:T(1,128)S(1)}, u32[]{:S(2)}, u32[]{:S(2)}) collective-permute-start(f32[3,16,1,128]{3,2,1,0:T(1,128)S(1)} %get-tuple-element.60), channel_id=1, source_target_pairs={{8,0},{16,8},{24,16},{9,1},{17,9},{25,17},{10,2},{18,10},{26,18},{... | collective-permute-start | bytes 73736 | tf_op jit(solution)/shard_map/ppermute | solution.py:30
  36.0 7.0 %collective-permute-start.9 = (f32[3,16,1,128]{3,2,1,0:T(1,128)S(1)}, f32[3,16,1,128]{3,2,1,0:T(1,128)S(1)}, u32[]{:S(2)}, u32[]{:S(2)}) collective-permute-start(f32[3,16,1,128]{3,2,1,0:T(1,128)S(1)} %get-tuple-element.59), channel_id=1, source_target_pairs={{0,8},{8,16},{16,24},{1,9},{9,17},{17,25},{2,10},{10,18},{18,26},{... | collective-permute-start | bytes 73736 | tf_op jit(solution)/shard_map/ppermute | solution.py:28
  43.1 0.6 copy-start.9
  43.7 0.6 copy-start.11
  45.0 6.1 %collective-permute-start.10 = (f32[3,16,18,1]{2,1,3,0:T(8,128)S(1)}, f32[3,16,18,1]{2,1,3,0:T(8,128)S(1)}, u32[]{:S(2)}, u32[]{:S(2)}) collective-permute-start(f32[3,16,18,1]{2,1,3,0:T(8,128)S(1)} %copy.20), channel_id=1, source_target_pairs={{1,0},{2,1},{3,2},{4,3},{5,4},{6,5},{7,6},{9,8},{10,9},{11,10},{12... | collective-permute-start | bytes 10376 | tf_op jit(solution)/shard_map/ppermute | solution.py:30
  46.9 5.4 %copy-start.10 = (f32[3,16,1,128]{3,2,1,0:T(1,128)S(1)}, f32[3,16,1,128]{3,2,1,0:T(1,128)}, u32[]{:S(2)}) copy-start(f32[3,16,1,128]{3,2,1,0:T(1,128)} %copy-done.9) | copy-start | bytes 73732
  46.9 5.4 %copy-start.12 = (f32[3,16,1,128]{3,2,1,0:T(1,128)S(1)}, f32[3,16,1,128]{3,2,1,0:T(1,128)}, u32[]{:S(2)}) copy-start(f32[3,16,1,128]{3,2,1,0:T(1,128)} %copy-done.11) | copy-start | bytes 73732
  47.3 4.6 %collective-permute-start.11 = (f32[3,16,18,1]{2,1,3,0:T(8,128)S(1)}, f32[3,16,18,1]{2,1,3,0:T(8,128)S(1)}, u32[]{:S(2)}, u32[]{:S(2)}) collective-permute-start(f32[3,16,18,1]{2,1,3,0:T(8,128)S(1)} %copy.22), channel_id=1, source_target_pairs={{0,1},{1,2},{2,3},{3,4},{4,5},{5,6},{6,7},{8,9},{9,10},{10,11},{11... | collective-permute-start | bytes 10376 | tf_op jit(solution)/shard_map/ppermute | solution.py:28
  51.5 1.3 copy-start.6
  52.8 18.3 %copy-start.4 = (s32[2,32,144]{2,1,0:T(8,128)S(1)}, s32[2,32,144]{2,1,0:T(8,128)}, u32[]{:S(2)}) copy-start(s32[2,32,144]{2,1,0:T(8,128)} %copy-done.3) | copy-start | bytes 110596
  54.4 5.9 %collective-permute-start.12 = (f32[5,8,128]{2,1,0:T(8,128)S(1)}, f32[5,8,128]{2,1,0:T(8,128)S(1)}, u32[]{:S(2)}, u32[]{:S(2)}) collective-permute-start(f32[5,8,128]{2,1,0:T(8,128)S(1)} %get-tuple-element.123), channel_id=1, source_target_pairs={{0,8},{8,16},{16,24},{1,9},{9,17},{17,25},{2,10},{10,18},{18,26},{... | collective-permute-start | bytes 61448 | tf_op jit(solution)/shard_map/ppermute | solution.py:28
  58.9 4.5 %collective-permute-start.13 = (f32[5,8,128]{2,1,0:T(8,128)S(1)}, f32[5,8,128]{2,1,0:T(8,128)S(1)}, u32[]{:S(2)}, u32[]{:S(2)}) collective-permute-start(f32[5,8,128]{2,1,0:T(8,128)S(1)} %get-tuple-element.124), channel_id=1, source_target_pairs={{8,0},{16,8},{24,16},{9,1},{17,9},{25,17},{10,2},{18,10},{26,18},{... | collective-permute-start | bytes 61448 | tf_op jit(solution)/shard_map/ppermute | solution.py:30
  63.6 7.6 %collective-permute-start.14 = (f32[5,32,8]{2,1,0:T(8,128)S(1)}, f32[5,32,8]{2,1,0:T(8,128)S(1)}, u32[]{:S(2)}, u32[]{:S(2)}) collective-permute-start(f32[5,32,8]{2,1,0:T(8,128)S(1)} %get-tuple-element.113), channel_id=1, source_target_pairs={{0,1},{1,2},{2,3},{3,4},{4,5},{5,6},{6,7},{8,9},{9,10},{10,11},{11... | collective-permute-start | bytes 15368 | tf_op jit(solution)/shard_map/ppermute | solution.py:28
  69.2 5.8 %collective-permute-start.15 = (f32[5,32,8]{2,1,0:T(8,128)S(1)}, f32[5,32,8]{2,1,0:T(8,128)S(1)}, u32[]{:S(2)}, u32[]{:S(2)}) collective-permute-start(f32[5,32,8]{2,1,0:T(8,128)S(1)} %get-tuple-element.114), channel_id=1, source_target_pairs={{1,0},{2,1},{3,2},{4,3},{5,4},{6,5},{7,6},{9,8},{10,9},{11,10},{12... | collective-permute-start | bytes 15368 | tf_op jit(solution)/shard_map/ppermute | solution.py:30
  76.3 5.6 %collective-permute-start.16 = (f32[5,8,128]{2,1,0:T(8,128)S(1)}, f32[5,8,128]{2,1,0:T(8,128)S(1)}, u32[]{:S(2)}, u32[]{:S(2)}) collective-permute-start(f32[5,8,128]{2,1,0:T(8,128)S(1)} %get-tuple-element.121), channel_id=1, source_target_pairs={{0,8},{8,16},{16,24},{1,9},{9,17},{17,25},{2,10},{10,18},{18,26},{... | collective-permute-start | bytes 61448 | tf_op jit(solution)/shard_map/ppermute | solution.py:28
  80.6 4.5 %collective-permute-start.17 = (f32[5,8,128]{2,1,0:T(8,128)S(1)}, f32[5,8,128]{2,1,0:T(8,128)S(1)}, u32[]{:S(2)}, u32[]{:S(2)}) collective-permute-start(f32[5,8,128]{2,1,0:T(8,128)S(1)} %get-tuple-element.122), channel_id=1, source_target_pairs={{8,0},{16,8},{24,16},{9,1},{17,9},{25,17},{10,2},{18,10},{26,18},{... | collective-permute-start | bytes 61448 | tf_op jit(solution)/shard_map/ppermute | solution.py:30
  85.2 6.0 %collective-permute-start.18 = (f32[5,32,8]{2,1,0:T(8,128)S(1)}, f32[5,32,8]{2,1,0:T(8,128)S(1)}, u32[]{:S(2)}, u32[]{:S(2)}) collective-permute-start(f32[5,32,8]{2,1,0:T(8,128)S(1)} %get-tuple-element.111), channel_id=1, source_target_pairs={{0,1},{1,2},{2,3},{3,4},{4,5},{5,6},{6,7},{8,9},{9,10},{10,11},{11... | collective-permute-start | bytes 15368 | tf_op jit(solution)/shard_map/ppermute | solution.py:28
  88.5 5.8 %collective-permute-start.19 = (f32[5,32,8]{2,1,0:T(8,128)S(1)}, f32[5,32,8]{2,1,0:T(8,128)S(1)}, u32[]{:S(2)}, u32[]{:S(2)}) collective-permute-start(f32[5,32,8]{2,1,0:T(8,128)S(1)} %get-tuple-element.112), channel_id=1, source_target_pairs={{1,0},{2,1},{3,2},{4,3},{5,4},{6,5},{7,6},{9,8},{10,9},{11,10},{12... | collective-permute-start | bytes 15368 | tf_op jit(solution)/shard_map/ppermute | solution.py:30
  97.0 3.9 %collective-permute-start.20 = (f32[3,16,1,128]{3,2,1,0:T(1,128)S(1)}, f32[3,16,1,128]{3,2,1,0:T(1,128)S(1)}, u32[]{:S(2)}, u32[]{:S(2)}) collective-permute-start(f32[3,16,1,128]{3,2,1,0:T(1,128)S(1)} %get-tuple-element.57), channel_id=1, source_target_pairs={{0,8},{8,16},{16,24},{1,9},{9,17},{17,25},{2,10},{10,18},{18,26},{... | collective-permute-start | bytes 73736 | tf_op jit(solution)/shard_map/ppermute | solution.py:28
  99.5 4.6 %collective-permute-start.21 = (f32[3,16,1,128]{3,2,1,0:T(1,128)S(1)}, f32[3,16,1,128]{3,2,1,0:T(1,128)S(1)}, u32[]{:S(2)}, u32[]{:S(2)}) collective-permute-start(f32[3,16,1,128]{3,2,1,0:T(1,128)S(1)} %get-tuple-element.58), channel_id=1, source_target_pairs={{8,0},{16,8},{24,16},{9,1},{17,9},{25,17},{10,2},{18,10},{26,18},{... | collective-permute-start | bytes 73736 | tf_op jit(solution)/shard_map/ppermute | solution.py:30
  104.8 5.6 %collective-permute-start.22 = (f32[3,16,18,1]{2,1,3,0:T(8,128)S(1)}, f32[3,16,18,1]{2,1,3,0:T(8,128)S(1)}, u32[]{:S(2)}, u32[]{:S(2)}) collective-permute-start(f32[3,16,18,1]{2,1,3,0:T(8,128)S(1)} %copy.24), channel_id=1, source_target_pairs={{0,1},{1,2},{2,3},{3,4},{4,5},{5,6},{6,7},{8,9},{9,10},{10,11},{11... | collective-permute-start | bytes 10376 | tf_op jit(solution)/shard_map/ppermute | solution.py:28
  108.4 5.1 %collective-permute-start.23 = (f32[3,16,18,1]{2,1,3,0:T(8,128)S(1)}, f32[3,16,18,1]{2,1,3,0:T(8,128)S(1)}, u32[]{:S(2)}, u32[]{:S(2)}) collective-permute-start(f32[3,16,18,1]{2,1,3,0:T(8,128)S(1)} %copy.25), channel_id=1, source_target_pairs={{1,0},{2,1},{3,2},{4,3},{5,4},{6,5},{7,6},{9,8},{10,9},{11,10},{12... | collective-permute-start | bytes 10376 | tf_op jit(solution)/shard_map/ppermute | solution.py:30
  114.6 7.1 %collective-permute-start.24 = (f32[3,16,1,128]{3,2,1,0:T(1,128)S(1)}, f32[3,16,1,128]{3,2,1,0:T(1,128)S(1)}, u32[]{:S(2)}, u32[]{:S(2)}) collective-permute-start(f32[3,16,1,128]{3,2,1,0:T(1,128)S(1)} %get-tuple-element.56), channel_id=1, source_target_pairs={{8,0},{16,8},{24,16},{9,1},{17,9},{25,17},{10,2},{18,10},{26,18},{... | collective-permute-start | bytes 73736 | tf_op jit(solution)/shard_map/ppermute | solution.py:30
  115.9 5.8 %collective-permute-start.25 = (f32[3,16,1,128]{3,2,1,0:T(1,128)S(1)}, f32[3,16,1,128]{3,2,1,0:T(1,128)S(1)}, u32[]{:S(2)}, u32[]{:S(2)}) collective-permute-start(f32[3,16,1,128]{3,2,1,0:T(1,128)S(1)} %get-tuple-element.55), channel_id=1, source_target_pairs={{0,8},{8,16},{16,24},{1,9},{9,17},{17,25},{2,10},{10,18},{18,26},{... | collective-permute-start | bytes 73736 | tf_op jit(solution)/shard_map/ppermute | solution.py:28
  122.3 6.2 %collective-permute-start.26 = (f32[3,16,18,1]{2,1,3,0:T(8,128)S(1)}, f32[3,16,18,1]{2,1,3,0:T(8,128)S(1)}, u32[]{:S(2)}, u32[]{:S(2)}) collective-permute-start(f32[3,16,18,1]{2,1,3,0:T(8,128)S(1)} %copy.30), channel_id=1, source_target_pairs={{1,0},{2,1},{3,2},{4,3},{5,4},{6,5},{7,6},{9,8},{10,9},{11,10},{12... | collective-permute-start | bytes 10376 | tf_op jit(solution)/shard_map/ppermute | solution.py:30
  124.6 4.6 %collective-permute-start.27 = (f32[3,16,18,1]{2,1,3,0:T(8,128)S(1)}, f32[3,16,18,1]{2,1,3,0:T(8,128)S(1)}, u32[]{:S(2)}, u32[]{:S(2)}) collective-permute-start(f32[3,16,18,1]{2,1,3,0:T(8,128)S(1)} %copy.32), channel_id=1, source_target_pairs={{0,1},{1,2},{2,3},{3,4},{4,5},{5,6},{6,7},{8,9},{9,10},{10,11},{11... | collective-permute-start | bytes 10376 | tf_op jit(solution)/shard_map/ppermute | solution.py:28
  129.0 1.1 copy-start.7
  132.3 4.8 %collective-permute-start.28 = (f32[5,8,128]{2,1,0:T(8,128)S(1)}, f32[5,8,128]{2,1,0:T(8,128)S(1)}, u32[]{:S(2)}, u32[]{:S(2)}) collective-permute-start(f32[5,8,128]{2,1,0:T(8,128)S(1)} %get-tuple-element.119), channel_id=1, source_target_pairs={{0,8},{8,16},{16,24},{1,9},{9,17},{17,25},{2,10},{10,18},{18,26},{... | collective-permute-start | bytes 61448 | tf_op jit(solution)/shard_map/ppermute | solution.py:28
  135.7 4.9 %collective-permute-start.29 = (f32[5,8,128]{2,1,0:T(8,128)S(1)}, f32[5,8,128]{2,1,0:T(8,128)S(1)}, u32[]{:S(2)}, u32[]{:S(2)}) collective-permute-start(f32[5,8,128]{2,1,0:T(8,128)S(1)} %get-tuple-element.120), channel_id=1, source_target_pairs={{8,0},{16,8},{24,16},{9,1},{17,9},{25,17},{10,2},{18,10},{26,18},{... | collective-permute-start | bytes 61448 | tf_op jit(solution)/shard_map/ppermute | solution.py:30
  140.7 7.3 %collective-permute-start.30 = (f32[5,32,8]{2,1,0:T(8,128)S(1)}, f32[5,32,8]{2,1,0:T(8,128)S(1)}, u32[]{:S(2)}, u32[]{:S(2)}) collective-permute-start(f32[5,32,8]{2,1,0:T(8,128)S(1)} %get-tuple-element.109), channel_id=1, source_target_pairs={{0,1},{1,2},{2,3},{3,4},{4,5},{5,6},{6,7},{8,9},{9,10},{10,11},{11... | collective-permute-start | bytes 15368 | tf_op jit(solution)/shard_map/ppermute | solution.py:28
  146.1 5.8 %collective-permute-start.31 = (f32[5,32,8]{2,1,0:T(8,128)S(1)}, f32[5,32,8]{2,1,0:T(8,128)S(1)}, u32[]{:S(2)}, u32[]{:S(2)}) collective-permute-start(f32[5,32,8]{2,1,0:T(8,128)S(1)} %get-tuple-element.110), channel_id=1, source_target_pairs={{1,0},{2,1},{3,2},{4,3},{5,4},{6,5},{7,6},{9,8},{10,9},{11,10},{12... | collective-permute-start | bytes 15368 | tf_op jit(solution)/shard_map/ppermute | solution.py:30
  153.2 5.8 %collective-permute-start.32 = (f32[5,8,128]{2,1,0:T(8,128)S(1)}, f32[5,8,128]{2,1,0:T(8,128)S(1)}, u32[]{:S(2)}, u32[]{:S(2)}) collective-permute-start(f32[5,8,128]{2,1,0:T(8,128)S(1)} %get-tuple-element.117), channel_id=1, source_target_pairs={{0,8},{8,16},{16,24},{1,9},{9,17},{17,25},{2,10},{10,18},{18,26},{... | collective-permute-start | bytes 61448 | tf_op jit(solution)/shard_map/ppermute | solution.py:28
  157.7 4.5 %collective-permute-start.33 = (f32[5,8,128]{2,1,0:T(8,128)S(1)}, f32[5,8,128]{2,1,0:T(8,128)S(1)}, u32[]{:S(2)}, u32[]{:S(2)}) collective-permute-start(f32[5,8,128]{2,1,0:T(8,128)S(1)} %get-tuple-element.118), channel_id=1, source_target_pairs={{8,0},{16,8},{24,16},{9,1},{17,9},{25,17},{10,2},{18,10},{26,18},{... | collective-permute-start | bytes 61448 | tf_op jit(solution)/shard_map/ppermute | solution.py:30
  162.3 5.2 %collective-permute-start.34 = (f32[5,32,8]{2,1,0:T(8,128)S(1)}, f32[5,32,8]{2,1,0:T(8,128)S(1)}, u32[]{:S(2)}, u32[]{:S(2)}) collective-permute-start(f32[5,32,8]{2,1,0:T(8,128)S(1)} %get-tuple-element.107), channel_id=1, source_target_pairs={{0,1},{1,2},{2,3},{3,4},{4,5},{5,6},{6,7},{8,9},{9,10},{10,11},{11... | collective-permute-start | bytes 15368 | tf_op jit(solution)/shard_map/ppermute | solution.py:28
  165.6 5.8 %collective-permute-start.35 = (f32[5,32,8]{2,1,0:T(8,128)S(1)}, f32[5,32,8]{2,1,0:T(8,128)S(1)}, u32[]{:S(2)}, u32[]{:S(2)}) collective-permute-start(f32[5,32,8]{2,1,0:T(8,128)S(1)} %get-tuple-element.108), channel_id=1, source_target_pairs={{1,0},{2,1},{3,2},{4,3},{5,4},{6,5},{7,6},{9,8},{10,9},{11,10},{12... | collective-permute-start | bytes 15368 | tf_op jit(solution)/shard_map/ppermute | solution.py:30
  173.9 2.7 %copy-start.15 = (f32[16,128]{1,0:T(8,128)}, f32[16,128]{1,0:T(8,128)S(1)}, u32[]{:S(2)}) copy-start(f32[16,128]{1,0:T(8,128)S(1)} %get-tuple-element.20) | copy-start | bytes 24580
where the time goes:
time: 178 us; the launch traced here: 177 us
  starting transfers between devices  101 us (57%)
  waiting for transfers between devices  39.3 us (22%)
  other arithmetic  21.1 us (12%)
  local copies, waits for them, and re-layouts  13.8 us (8%)
  between operations  1.78 us (1%)
    ppermute x18, starting transfers between devices, padded(): lax.ppermute(tail, axis, [(i, (i + 1) % count) for i in range(ends)])  71.3 us
    ppermute x18, waiting for transfers between devices, padded(): lax.ppermute(head, axis, [((i + 1) % count, i) for i in range(ends)])  38.6 us
    ppermute x18, starting transfers between devices, padded(): lax.ppermute(head, axis, [((i + 1) % count, i) for i in range(ends)])  29.4 us
    unnamed x40, local copies, waits for them, and re-layouts  3.72 us
  transfers between devices with their start and end apart: 36, of which 14 were waited for; matrix products, arithmetic and copies ran while one was open for 7% of the time, Pallas kernels for 0%

commit v1 on v0

v1 whole, which is shorter than its diff:
```python
import jax
import jax.numpy as jnp
from jax import lax
from jax.experimental import pallas as pl
from jax.experimental.pallas import tpu as pltpu
from jax.sharding import PartitionSpec as P

SUB = 8
STEPS = 2
LANES = 128
ROWS = 16
LEVELS = 16
FIELDS = 3
STACK = FIELDS * LEVELS
MESH = pl.DeviceIdType.MESH
F32 = jnp.float32

DIRS = [(-1, 0), (1, 0), (0, -1), (0, 1), (-1, -1), (-1, 1), (1, -1), (1, 1)]
SIDES = [(-1, -1), (0, -1), (1, -1), (-1, 1), (0, 1), (1, 1)]
FAR = STACK
FLAT = 2 * STACK


def turn(x, shift, axis):
    return pltpu.roll(x, shift % x.shape[axis] if isinstance(shift, int) else shift, axis)


def kernel(
    vel_u, vel_v, buoy, surface, trans_u, trans_v, ocean, layers,
    out_u, out_v, out_b, out_eta, out_tu, out_tv,
    fx, lp, dyb, star_u, star_v, near_ext, code_ext,
    x_send, y_send, x_recv, y_recv, fx_send, fy_send, fx_recv, fy_recv,
    send_sem, recv_sem,
):
    gx, gy = lax.axis_index("gx"), lax.axis_index("gy")
    nx, ny = lax.axis_size("gx"), lax.axis_size("gy")

    def exists(d):
        ok = jnp.bool_(True)
        if d[0] == -1:
            ok = jnp.logical_and(ok, gx > 0)
        if d[0] == 1:
            ok = jnp.logical_and(ok, gx < nx - 1)
        if d[1] == -1:
            ok = jnp.logical_and(ok, gy > 0)
        if d[1] == 1:
            ok = jnp.logical_and(ok, gy < ny - 1)
        return ok

    here = {d: exists(d) for d in DIRS}
    barrier = pltpu.get_barrier_semaphore()
    total_near = jnp.int32(0)
    for d in DIRS:
        total_near = total_near + here[d].astype(jnp.int32)

        @pl.when(here[d])
        def _(d=d):
            pl.semaphore_signal(barrier, inc=1, device_id=(gx + d[0], gy + d[1]), device_id_type=MESH)

    for d in DIRS:
        @pl.when(jnp.logical_not(here[d]))
        def _(d=d):
            for p in range(STEPS):
                if d[1] == 0:
                    s = 0 if d[0] < 0 else 1
                    x_recv[p, s] = jnp.zeros(x_recv.shape[2:], F32)
                    fx_recv[p, s] = jnp.zeros(fx_recv.shape[2:], F32)
                else:
                    s = SIDES.index(d)
                    y_recv[p, s] = jnp.zeros(y_recv.shape[2:], F32)
                    fy_recv[p, s] = jnp.zeros(fy_recv.shape[2:], F32)

    def copies(phase, step):
        result = []
        for i, d in enumerate(DIRS):
            back = (-d[0], -d[1])
            if d[1] == 0:
                src_at, dst_at = (0 if d[0] < 0 else 1), (0 if back[0] < 0 else 1)
                if phase == 0:
                    src, dst = x_send.at[step, src_at], x_recv.at[step, dst_at]
                    if step:
                        short = FLAT + 3 * ROWS
                        src, dst = src.at[pl.ds(0, short)], dst.at[pl.ds(0, short)]
                else:
                    src, dst = fx_send.at[step], fx_recv.at[step, dst_at]
            else:
                src_at, dst_at = (0 if d[1] < 0 else 1), SIDES.index(back)
                if phase == 0:
                    src, dst = y_send.at[step, src_at], y_recv.at[step, dst_at]
                else:
                    src, dst = fy_send.at[step, src_at], fy_recv.at[step, dst_at]
            at = phase * STEPS + step
            copy = pltpu.make_async_remote_copy(
                src_ref=src, dst_ref=dst,
                send_sem=send_sem.at[at, i], recv_sem=recv_sem.at[at, DIRS.index(back)],
                device_id=(gx + d[0], gy + d[1]), device_id_type=MESH,
            )
            result.append((d, copy))
        return result

    def start(phase, step):
        for d, copy in copies(phase, step):
            @pl.when(here[d])
            def _(copy=copy):
                copy.start()

    def arrive(phase, step):
        by_dir = dict(copies(phase, step))
        for d in DIRS:
            @pl.when(here[d])
            def _(d=d):
                by_dir[(-d[0], -d[1])].wait_recv()

    def sent(phase, step):
        for d, copy in copies(phase, step):
            @pl.when(here[d])
            def _(copy=copy):
                copy.wait_send()

    lane = lax.broadcasted_iota(jnp.int32, (ROWS, LANES), 1)
    pair = lane >> 1
    odd = (lane & 1) == 1
    zero = jnp.zeros((ROWS, LANES), F32)

    def put(step, j, cells, strips):
        fx[j, pl.ds(2, ROWS)] = cells
        x_send[step, 0, pl.ds(j, 1)] = cells[0:1]
        x_send[step, 0, pl.ds(FAR + j, 1)] = cells[1:2]
        x_send[step, 1, pl.ds(j, 1)] = cells[ROWS - 1 : ROWS]
        x_send[step, 1, pl.ds(FAR + j, 1)] = cells[ROWS - 2 : ROWS - 1]
        to_left, to_right = strips
        rolled = pltpu.roll(cells, 2 * j + 2, 1)
        to_right = jnp.where(pair == j, rolled, to_right)
        to_left = jnp.where(pair == j + 1, rolled, to_left)
        return to_left, to_right

    def pack_flat(arrays):
        to_left, to_right = zero, zero
        for a, cells in enumerate(arrays):
            rolled = turn(cells, 16 * a + 16, 1)
            to_right = jnp.where((lane >> 4) == a, rolled, to_right)
            to_left = jnp.where((lane >> 4) == a + 1, rolled, to_left)
        return to_left, to_right

    def send_state(step, strips, flats):
        y_send[step, 0, 0:ROWS] = strips[0]
        y_send[step, 1, 0:ROWS] = strips[1]
        flat_left, flat_right = pack_flat(flats)
        y_send[step, 0, ROWS : 2 * ROWS] = flat_left
        y_send[step, 1, ROWS : 2 * ROWS] = flat_right
        for s in range(2):
            for a, cells in enumerate(flats):
                x_send[step, s, FLAT + ROWS * a : FLAT + ROWS * (a + 1)] = cells
        start(0, step)

    def side_of(from_left, from_right, a):
        cells = jnp.where(
            (lane >> 4) == a + 1, from_right, jnp.where((lane >> 4) == a, from_left, 0.0)
        )
        return turn(cells, -(16 * a + 16), 1)

    def wide(own, up, down, sides, a):
        main = jnp.concatenate([up, own, down], axis=0)
        side = jnp.concatenate([side_of(sides[r], sides[r + 3], a) for r in range(3)], axis=0)
        return jnp.concatenate([main, side], axis=1)

    lay = layers[...].astype(F32)
    code = jnp.where(ocean[...] > 0, lay, 0.0)

    strips = (zero, zero)
    for a, ref in enumerate((vel_u, vel_v, buoy)):
        def pack(k, strips, a=a, ref=ref):
            return put(0, a * LEVELS + k, ref[k], strips)

        strips = lax.fori_loop(0, LEVELS, pack, strips, unroll=True)
    pl.semaphore_wait(barrier, total_near)
    sea, flow_u, flow_v = surface[...], trans_u[...], trans_v[...]
    send_state(0, strips, (sea, flow_u, flow_v, code))

    lane18 = lax.broadcasted_iota(jnp.int32, (ROWS + 2, LANES), 1)
    for step in range(STEPS):
        arrive(0, step)
        from_left, from_right = y_recv[step, 1, 0:ROWS], y_recv[step, 4, 0:ROWS]
        near = jnp.where(odd, from_left, turn(from_right, -2, 1))
        far = jnp.where(odd, turn(from_left, 1, 1), turn(from_right, -3, 1))
        inner = turn(jnp.where(odd, strips[1], strips[0]), -1, 1)
        near_ext[pl.ds(1, ROWS)] = near
        odd8 = odd[0:8]
        top = jnp.where(odd8, y_recv[step, 0, 8:16], turn(y_recv[step, 3, 8:16], -2, 1))
        low = jnp.where(odd8, y_recv[step, 2, 0:8], turn(y_recv[step, 5, 0:8], -2, 1))
        near_ext[pl.ds(0, 1)] = top[7:8]
        near_ext[pl.ds(ROWS + 1, 1)] = low[0:1]

        flats_y = [y_recv[step, r, ROWS : 2 * ROWS] for r in range(6)]

        def flat_x(s, a):
            return x_recv[step, s, FLAT + ROWS * a : FLAT + ROWS * (a + 1)]

        if step == 0:
            code_wide = wide(code, flat_x(0, 3), flat_x(1, 3), flats_y, 3)
            code_ext[...] = code_wide[:, 0:LANES]
            code_side = code_wide[ROWS : 2 * ROWS, LANES:]
            code_near = jnp.where(
                odd,
                jnp.broadcast_to(code_side[:, LANES - 1 : LANES], (ROWS, LANES)),
                jnp.broadcast_to(code_side[:, 0:1], (ROWS, LANES)),
            )
            act_near = ((pair & (LEVELS - 1)).astype(F32) < code_near).astype(F32)
        lap_near = act_near * (
            far + inner + near_ext[pl.ds(0, ROWS)] + near_ext[pl.ds(2, ROWS)] - 4.0 * near
        )
        near18 = near_ext[pl.ds(0, ROWS + 2)]
        code18 = code_ext[pl.ds(ROWS - 1, ROWS + 2)]

        def biharm(j, act18, keep):
            fx[j, pl.ds(0, 1)] = x_recv[step, 0, pl.ds(FAR + j, 1)]
            fx[j, pl.ds(1, 1)] = x_recv[step, 0, pl.ds(j, 1)]
            fx[j, pl.ds(ROWS + 2, 1)] = x_recv[step, 1, pl.ds(j, 1)]
            fx[j, pl.ds(ROWS + 3, 1)] = x_recv[step, 1, pl.ds(FAR + j, 1)]
            mid = fx[j, pl.ds(1, ROWS + 2)]
            edge = pltpu.roll(near18, 127 - 2 * j, 1)
            ahead = jnp.where(lane18 == LANES - 1, edge, turn(mid, -1, 1))
            behind = jnp.where(lane18 == 0, edge, turn(mid, 1, 1))
            lap = act18 * (
                fx[j, pl.ds(0, ROWS + 2)] + fx[j, pl.ds(2, ROWS + 2)] + ahead + behind - 4.0 * mid
            )
            lp[j, pl.ds(0, ROWS + 2)] = lap
            if keep is not None:
                dyb[keep, pl.ds(0, ROWS + 2)] = ahead - behind
            mid = lp[j, pl.ds(1, ROWS)]
            edge = pltpu.roll(lap_near, 127 - 2 * j, 1)
            ahead = jnp.where(lane == LANES - 1, edge, turn(mid, -1, 1))
            behind = jnp.where(lane == 0, edge, turn(mid, 1, 1))
            return lp[j, pl.ds(0, ROWS)] + lp[j, pl.ds(2, ROWS)] + ahead + behind - 4.0 * mid

        def level(k, carry):
            press_x, press_y, force_u, force_v, col_u, col_v = carry
            level_at = lax.convert_element_type(k, F32)
            act18 = (level_at < code18).astype(F32)
            act = (level_at < code).astype(F32)
            bih_u = biharm(k, act18, None)
            bih_v = biharm(LEVELS + k, act18, None)
            bih_b = biharm(2 * LEVELS + k, act18, k)
            u, v = fx[k, pl.ds(2, ROWS)], fx[LEVELS + k, pl.ds(2, ROWS)]
            at = 2 * LEVELS + k
            b = fx[at, pl.ds(2, ROWS)]
            b_x = fx[at, pl.ds(3, ROWS)] - fx[at, pl.ds(1, ROWS)]
            b_y = dyb[k, pl.ds(1, ROWS)]
            press_x, press_y = press_x + b_x, press_y + b_y
            tend_u = (-0.25 / LEVELS) * press_x + 0.1 * v - 0.02 * bih_u
            tend_v = (-0.25 / LEVELS) * press_y - 0.1 * u - 0.02 * bih_v
            tend_b = -0.5 * (u * b_x + v * b_y) - 0.02 * bih_b
            su = act * (u + 0.2 * tend_u)
            sv = act * (v + 0.2 * tend_v)
            star_u[k] = su
            star_v[k] = sv
            new_b = act * (b + 0.2 * tend_b)
            if step == STEPS - 1:
                out_b[k] = new_b
            else:
                fx[at, pl.ds(2, ROWS)] = new_b
            return (
                press_x, press_y, force_u + act * tend_u, force_v + act * tend_v,
                col_u + su, col_v + sv,
            )

        _, _, force_u, force_v, col_u, col_v = lax.fori_loop(
            0, LEVELS, level, (zero,) * 6, unroll=True
        )
        force_u, force_v = force_u / LEVELS, force_v / LEVELS
        fx_send[step, 0:ROWS] = force_u
        fx_send[step, ROWS : 2 * ROWS] = force_v
        flat_left, flat_right = pack_flat((force_u, force_v))
        fy_send[step, 0] = flat_left
        fy_send[step, 1] = flat_right
        start(1, step)

        wet = (code_wide > 0.0).astype(F32)
        depth = code_wide / LEVELS
        state = tuple(
            wide(own, flat_x(0, a), flat_x(1, a), flats_y, a)
            for a, own in enumerate((sea, flow_u, flow_v))
        )
        if step < STEPS - 1:
            def pack_b(k, strips):
                j = 2 * LEVELS + k
                return put(step + 1, j, fx[j, pl.ds(2, ROWS)], strips)

            strips = lax.fori_loop(0, LEVELS, pack_b, (zero, zero), unroll=True)
        arrive(1, step)
        sides = [fy_recv[step, r] for r in range(6)]
        push_u, push_v = (
            0.2 * wide(
                own, fx_recv[step, 0, ROWS * a : ROWS * (a + 1)],
                fx_recv[step, 1, ROWS * a : ROWS * (a + 1)], sides, a,
            )
            for a, own in enumerate((force_u, force_v))
        )

        def substep(_, carry):
            eta, tu, tv, sum_u, sum_v = carry
            div = (turn(tu, -1, 0) - turn(tu, 1, 0)) + (turn(tv, -1, 1) - turn(tv, 1, 1))
            eta = wet * (eta - 0.125 * div)
            thick = 0.125 * (depth + eta)
            new_u = wet * (
                0.98 * tu + push_u - thick * (turn(eta, -1, 0) - turn(eta, 1, 0)) + 0.05 * tv
            )
            new_v = wet * (
                0.98 * tv + push_v - thick * (turn(eta, -1, 1) - turn(eta, 1, 1)) - 0.05 * tu
            )
            sum_u = sum_u + new_u[ROWS : 2 * ROWS, 0:LANES]
            sum_v = sum_v + new_v[ROWS : 2 * ROWS, 0:LANES]
            return eta, new_u, new_v, sum_u, sum_v

        eta, tu, tv, sum_u, sum_v = lax.fori_loop(0, SUB, substep, state + (zero, zero))
        sea, flow_u, flow_v = (c[ROWS : 2 * ROWS, 0:LANES] for c in (eta, tu, tv))
        scale = LEVELS / SUB
        shift_u = (scale * sum_u - col_u) / lay
        shift_v = (scale * sum_v - col_v) / lay

        if step == STEPS - 1:
            def finish(k, carry):
                act = (lax.convert_element_type(k, F32) < code).astype(F32)
                out_u[k] = act * (star_u[k] + shift_u)
                out_v[k] = act * (star_v[k] + shift_v)
                return carry

            lax.fori_loop(0, LEVELS, finish, 0, unroll=True)
            out_eta[...] = sea
            out_tu[...] = flow_u
            out_tv[...] = flow_v
        else:
            def couple(k, strips):
                act = (lax.convert_element_type(k, F32) < code).astype(F32)
                strips = put(step + 1, k, act * (star_u[k] + shift_u), strips)
                return put(step + 1, LEVELS + k, act * (star_v[k] + shift_v), strips)

            strips = lax.fori_loop(0, LEVELS, couple, strips, unroll=True)
            send_state(step + 1, strips, (sea, flow_u, flow_v))

    for step in range(STEPS):
        sent(0, step)
        sent(1, step)


def per_device(velocity_u, velocity_v, buoyancy, surface, transport_u, transport_v, ocean, layers):
    cube = jax.ShapeDtypeStruct(velocity_u.shape, F32)
    flat = jax.ShapeDtypeStruct(surface.shape, F32)
    vmem = pl.BlockSpec(memory_space=pltpu.VMEM)
    ext = 24
    return tuple(
        pl.pallas_call(
            kernel,
            out_shape=(cube, cube, cube, flat, flat, flat),
            in_specs=[vmem] * 8,
            out_specs=(vmem,) * 6,
            scratch_shapes=[
                pltpu.VMEM((STACK, ext, LANES), F32),
                pltpu.VMEM((STACK, ext, LANES), F32),
                pltpu.VMEM((LEVELS, ext, LANES), F32),
                pltpu.VMEM((LEVELS, ROWS, LANES), F32),
                pltpu.VMEM((LEVELS, ROWS, LANES), F32),
                pltpu.VMEM((ext, LANES), F32),
                pltpu.VMEM((3 * ROWS, LANES), F32),
                pltpu.VMEM((STEPS, 2, FLAT + 4 * ROWS, LANES), F32),
                pltpu.VMEM((STEPS, 2, 2 * ROWS, LANES), F32),
                pltpu.VMEM((STEPS, 2, FLAT + 4 * ROWS, LANES), F32),
                pltpu.VMEM((STEPS, 6, 2 * ROWS, LANES), F32),
                pltpu.VMEM((STEPS, 2 * ROWS, LANES), F32),
                pltpu.VMEM((STEPS, 2, ROWS, LANES), F32),
                pltpu.VMEM((STEPS, 2, 2 * ROWS, LANES), F32),
                pltpu.VMEM((STEPS, 6, ROWS, LANES), F32),
                pltpu.SemaphoreType.DMA((2 * STEPS, 8)),
                pltpu.SemaphoreType.DMA((2 * STEPS, 8)),
            ],
            compiler_params=pltpu.CompilerParams(
                collective_id=0, has_side_effects=True, vmem_limit_bytes=24 * 2**20
            ),
        )(velocity_u, velocity_v, buoyancy, surface, transport_u, transport_v, ocean, layers)
    )


def solution(mesh):
    cube, flat = P(None, "gx", "gy"), P("gx", "gy")
    return jax.shard_map(
        per_device,
        mesh=mesh,
        in_specs=(cube, cube, cube, flat, flat, flat, flat, flat),
        out_specs=(cube, cube, cube, flat, flat, flat),
        check_vma=False,
    )
```

time: 178 us -> 46.3 us (0.26)
  starting transfers between devices: 101 us -> 0 us
  waiting for transfers between devices: 39.3 us -> 0 us
  Pallas kernels: 0 us -> 35.3 us
  other arithmetic: 21.1 us -> 0 us
  local copies, waits for them, and re-layouts: 13.8 us -> 9.95 us
    ppermute x36 -> x0, starting transfers between devices: 101 us -> none  [the longest x18 71.3 us: padded(): lax.ppermute(tail, axis, [(i, (i + 1) % count) for i in range(ends)])]
    ppermute x36 -> x0, waiting for transfers between devices: 39.3 us -> none  [the longest x18 38.6 us: padded(): lax.ppermute(head, axis, [((i + 1) % count, i) for i in range(ends)])]
    pallas_call x0 -> x1, Pallas kernels: none -> 35.3 us  [per_device(): pl.pallas_call(kernel, out_shape=(cube, cube, cube, flat, flat, flat), in...]
    mul x32 -> x0, other arithmetic: 6.38 us -> none  [the longest x1 1.96 us: couple_columns(): new_v = active * (star_v - column_v + total_v / substeps / column_depth)]
    unnamed x40 -> x22, local copies, waits for them, and re-layouts: 3.72 us -> 9.95 us
    slice x27 -> x0, local copies, waits for them, and re-layouts: 4.69 us -> none  [the longest x19 2.56 us: padded(): lax.slice_in_dim(cells, cells.shape[dim] - width, cells.shape[dim], axis=...]
    reduce_sum x2 -> x0, other arithmetic: 3.7 us -> none  [the longest x1 2.16 us: couple_columns(): column_v = jnp.sum(star_v, axis=0) / layer_count]
    another operation x10 -> x0, other arithmetic: 3.34 us -> none  [the longest x2 1.29 us: per_device(): stacked = jnp.stack([new_u, new_v, new_buoy])]
  transfers between devices with their start and end apart: 36 -> 0, of which waited for: 14 -> 0; matrix products, arithmetic and copies ran while one was open for 7% -> 0% of each run, Pallas kernels for 0% -> 0%
where the time goes in v1:
time: 46.3 us; the launch traced here: 45.9 us
  Pallas kernels  35.3 us (76%)
  local copies, waits for them, and re-layouts  9.95 us (21%)
  between operations  0.66 us (1%)
    pallas_call x1, Pallas kernels, per_device(): pl.pallas_call(kernel, out_shape=(cube, cube, cube, flat, flat, flat), in...  35.3 us
    unnamed x22, local copies, waits for them, and re-layouts  9.95 us

profile of v1, /device:TPU:1, one launch (start us, length us, event | category | flops | bytes accessed | tf_op | source)
XLA Modules:
  0.0 45.9 jit_solution(15921934718732833744)
XLA Ops:
  0.6 0.0 copy-start
  0.6 0.9 %copy-done = f32[16,16,128]{2,1,0:T(8,128)S(1)} copy-done((f32[16,16,128]{2,1,0:T(8,128)S(1)}, f32[16,16,128]{2,1,0:T(8,128)}, u32[]{:S(2)}) %copy-start) | copy-done | bytes 131096
  1.5 0.0 copy-start.1
  1.5 0.9 %copy-done.1 = f32[16,16,128]{2,1,0:T(8,128)S(1)} copy-done((f32[16,16,128]{2,1,0:T(8,128)S(1)}, f32[16,16,128]{2,1,0:T(8,128)}, u32[]{:S(2)}) %copy-start.1) | copy-done | bytes 131096
  2.4 0.0 copy-start.2
  2.4 0.9 %copy-done.2 = f32[16,16,128]{2,1,0:T(8,128)S(1)} copy-done((f32[16,16,128]{2,1,0:T(8,128)S(1)}, f32[16,16,128]{2,1,0:T(8,128)}, u32[]{:S(2)}) %copy-start.2) | copy-done | bytes 131096
  3.3 0.0 copy-start.3
  3.4 0.7 %copy-done.3 = f32[16,128]{1,0:T(8,128)S(1)} copy-done((f32[16,128]{1,0:T(8,128)S(1)}, f32[16,128]{1,0:T(8,128)}, u32[]{:S(2)}) %copy-start.3) | copy-done | bytes 8216
  4.0 0.0 copy-start.4
  4.0 0.7 %copy-done.4 = f32[16,128]{1,0:T(8,128)S(1)} copy-done((f32[16,128]{1,0:T(8,128)S(1)}, f32[16,128]{1,0:T(8,128)}, u32[]{:S(2)}) %copy-start.4) | copy-done | bytes 8216
  4.7 0.0 copy-start.5
  4.7 0.7 %copy-done.5 = f32[16,128]{1,0:T(8,128)S(1)} copy-done((f32[16,128]{1,0:T(8,128)S(1)}, f32[16,128]{1,0:T(8,128)}, u32[]{:S(2)}) %copy-start.5) | copy-done | bytes 8216
  5.4 0.0 copy-start.6
  5.4 0.7 %copy-done.6 = s32[16,128]{1,0:T(8,128)S(1)} copy-done((s32[16,128]{1,0:T(8,128)S(1)}, s32[16,128]{1,0:T(8,128)}, u32[]{:S(2)}) %copy-start.6) | copy-done | bytes 8216
  6.1 0.0 copy-start.7
  6.1 0.7 %copy-done.7 = s32[16,128]{1,0:T(8,128)S(1)} copy-done((s32[16,128]{1,0:T(8,128)S(1)}, s32[16,128]{1,0:T(8,128)}, u32[]{:S(2)}) %copy-start.7) | copy-done | bytes 8216
  6.8 35.3 %shard_map.127 = (f32[16,16,128]{2,1,0:T(8,128)S(1)}, f32[16,16,128]{2,1,0:T(8,128)S(1)}, f32[16,16,128]{2,1,0:T(8,128)S(1)}, f32[16,128]{1,0:T(8,128)S(1)}, f32...) custom-call(f32[16,16,128]{2,1,0:T(8,128)S(1)} %copy-done, f32[16,16,128]{2,1,0:T(8,128)S(1)} %copy-done.1, ...), custom_call_target="tpu_custom_call" | custom-call | tf_op jit(solution)/shard_map/pallas_call | solution.py:352
  42.2 0.7 %copy.20 = f32[16,16,128]{2,1,0:T(8,128)} copy(f32[16,16,128]{2,1,0:T(8,128)S(1)} %get-tuple-element.12) | data formatting | bytes 262144
  42.8 0.7 %copy.21 = f32[16,16,128]{2,1,0:T(8,128)} copy(f32[16,16,128]{2,1,0:T(8,128)S(1)} %get-tuple-element.13) | data formatting | bytes 262144
  43.5 0.7 %copy.22 = f32[16,16,128]{2,1,0:T(8,128)} copy(f32[16,16,128]{2,1,0:T(8,128)S(1)} %get-tuple-element.14) | data formatting | bytes 262144
  44.1 0.6 %copy.23 = f32[16,128]{1,0:T(8,128)} copy(f32[16,128]{1,0:T(8,128)S(1)} %get-tuple-element.15) | data formatting | bytes 16384
  44.7 0.6 %copy.24 = f32[16,128]{1,0:T(8,128)} copy(f32[16,128]{1,0:T(8,128)S(1)} %get-tuple-element.16) | data formatting | bytes 16384
  45.3 0.6 %copy.25 = f32[16,128]{1,0:T(8,128)} copy(f32[16,128]{1,0:T(8,128)S(1)} %get-tuple-element.17) | data formatting | bytes 16384
Async XLA Ops:
  0.6 0.9 %copy-start = (f32[16,16,128]{2,1,0:T(8,128)S(1)}, f32[16,16,128]{2,1,0:T(8,128)}, u32[]{:S(2)}) copy-start(f32[16,16,128]{2,1,0:T(8,128)} %vel_u.1) | copy-start | bytes 393220
  1.5 0.9 %copy-start.1 = (f32[16,16,128]{2,1,0:T(8,128)S(1)}, f32[16,16,128]{2,1,0:T(8,128)}, u32[]{:S(2)}) copy-start(f32[16,16,128]{2,1,0:T(8,128)} %vel_v.1) | copy-start | bytes 393220
  2.4 0.9 %copy-start.2 = (f32[16,16,128]{2,1,0:T(8,128)S(1)}, f32[16,16,128]{2,1,0:T(8,128)}, u32[]{:S(2)}) copy-start(f32[16,16,128]{2,1,0:T(8,128)} %buoy.1) | copy-start | bytes 393220
  3.3 0.7 %copy-start.3 = (f32[16,128]{1,0:T(8,128)S(1)}, f32[16,128]{1,0:T(8,128)}, u32[]{:S(2)}) copy-start(f32[16,128]{1,0:T(8,128)} %surface.1) | copy-start | bytes 24580
  4.0 0.7 %copy-start.4 = (f32[16,128]{1,0:T(8,128)S(1)}, f32[16,128]{1,0:T(8,128)}, u32[]{:S(2)}) copy-start(f32[16,128]{1,0:T(8,128)} %trans_u.1) | copy-start | bytes 24580
  4.7 0.7 %copy-start.5 = (f32[16,128]{1,0:T(8,128)S(1)}, f32[16,128]{1,0:T(8,128)}, u32[]{:S(2)}) copy-start(f32[16,128]{1,0:T(8,128)} %trans_v.1) | copy-start | bytes 24580
  5.4 0.7 %copy-start.6 = (s32[16,128]{1,0:T(8,128)S(1)}, s32[16,128]{1,0:T(8,128)}, u32[]{:S(2)}) copy-start(s32[16,128]{1,0:T(8,128)} %ocean.1) | copy-start | bytes 24580
  6.1 0.7 %copy-start.7 = (s32[16,128]{1,0:T(8,128)S(1)}, s32[16,128]{1,0:T(8,128)}, u32[]{:S(2)}) copy-start(s32[16,128]{1,0:T(8,128)} %layers.1) | copy-start | bytes 24580

commit v2 on v1

v2 whole, which is shorter than its diff:
```python
import jax
import jax.numpy as jnp
from jax import lax
from jax.experimental import pallas as pl
from jax.experimental.pallas import tpu as pltpu
from jax.sharding import PartitionSpec as P

SUB = 8
STEPS = 2
LANES = 128
ROWS = 16
LEVELS = 16
FIELDS = 3
STACK = FIELDS * LEVELS
MESH = pl.DeviceIdType.MESH
F32 = jnp.float32

DIRS = [(-1, 0), (1, 0), (0, -1), (0, 1), (-1, -1), (-1, 1), (1, -1), (1, 1)]
SIDES = [(-1, -1), (0, -1), (1, -1), (-1, 1), (0, 1), (1, 1)]
MOVING = 2 * LEVELS
CODE_ROW = 2 * STACK
RIM = CODE_ROW + 8
HALF = LANES // 2


RIMS, FORCE, PLANE, EARLY = 0, 1, 2, 3


def turn(x, shift, axis):
    return pltpu.roll(x, shift % x.shape[axis] if isinstance(shift, int) else shift, axis)


def fold(cells):
    low = lax.broadcasted_iota(jnp.int32, (8, LANES), 1) < HALF
    return jnp.where(low, cells[0:8], turn(cells[8:16], HALF, 1))


def unfold(cells):
    return jnp.concatenate([cells, turn(cells, HALF, 1)], axis=0)


def pack_flat(arrays):
    lane = lax.broadcasted_iota(jnp.int32, (ROWS, LANES), 1)
    to_left = to_right = jnp.zeros((ROWS, LANES), F32)
    for a, cells in enumerate(arrays):
        to_right = jnp.where((lane >> 4) == a, turn(cells, 16 * a + 16, 1), to_right)
        to_left = jnp.where((lane >> 4) == a, turn(cells, 16 * a, 1), to_left)
    return fold(to_left), fold(to_right)


def wide(own, up, down, sides, a):
    lane = lax.broadcasted_iota(jnp.int32, (ROWS, LANES), 1)
    blocks = []
    for r in range(3):
        from_left, from_right = unfold(sides[r]), unfold(sides[r + 3])
        left, right = turn(from_left, 112 - 16 * a, 1), turn(from_right, -16 * a, 1)
        blocks.append(jnp.where(lane < 16, right, jnp.where(lane >= 112, left, 0.0)))
    main = jnp.concatenate([up, own, down], axis=0)
    return jnp.concatenate([main, jnp.concatenate(blocks, axis=0)], axis=1)


def barotropic(state, push_u, push_v, code_wide):
    wet = (code_wide > 0.0).astype(F32)
    depth = code_wide / LEVELS
    zero = jnp.zeros((ROWS, LANES), F32)

    def substep(_, carry):
        eta, tu, tv, sum_u, sum_v = carry
        div = (turn(tu, -1, 0) - turn(tu, 1, 0)) + (turn(tv, -1, 1) - turn(tv, 1, 1))
        eta = wet * (eta - 0.125 * div)
        thick = 0.125 * (depth + eta)
        new_u = wet * (
            0.98 * tu + push_u - thick * (turn(eta, -1, 0) - turn(eta, 1, 0)) + 0.05 * tv
        )
        new_v = wet * (
            0.98 * tv + push_v - thick * (turn(eta, -1, 1) - turn(eta, 1, 1)) - 0.05 * tu
        )
        sum_u = sum_u + new_u[ROWS : 2 * ROWS, 0:LANES]
        sum_v = sum_v + new_v[ROWS : 2 * ROWS, 0:LANES]
        return eta, new_u, new_v, sum_u, sum_v

    eta, tu, tv, sum_u, sum_v = lax.fori_loop(0, SUB, substep, state + (zero, zero))
    own = tuple(c[ROWS : 2 * ROWS, 0:LANES] for c in (eta, tu, tv))
    return own, sum_u, sum_v


def finish_kernel(
    hbm_u, hbm_v, new_b, hbm_columns, hbm_wide,
    out_u, out_v, out_b, out_eta, out_tu, out_tv,
    star_u, star_v, columns, wide_in, buf_u, buf_v, buf_flat, sem, in_sem,
):
    loads = [
        pltpu.make_async_copy(src, dst, in_sem.at[i])
        for i, (src, dst) in enumerate((
            (hbm_wide, wide_in), (hbm_columns, columns), (hbm_u, star_u), (hbm_v, star_v)
        ))
    ]
    for load in loads:
        load.start()
    copies = [pltpu.make_async_copy(new_b, out_b, sem.at[0])]
    copies[0].start()
    loads[0].wait()
    code_wide = wide_in[3]
    own, sum_u, sum_v = barotropic(
        (wide_in[0], wide_in[1], wide_in[2]), wide_in[4], wide_in[5], code_wide
    )
    for a, (cells, out) in enumerate(zip(own, (out_eta, out_tu, out_tv))):
        buf_flat[a] = cells
        copies.append(pltpu.make_async_copy(buf_flat.at[a], out, sem.at[1 + a]))
        copies[-1].start()
    code = code_wide[ROWS : 2 * ROWS, 0:LANES]
    lay = jnp.maximum(code, 1.0)
    scale = LEVELS / SUB
    for load in loads[1:]:
        load.wait()
    for a, (star, buf, out, total) in enumerate(
        ((star_u, buf_u, out_u, sum_u), (star_v, buf_v, out_v, sum_v))
    ):
        shift = (scale * total - columns[a]) / lay

        def finish(k, carry, star=star, buf=buf, shift=shift):
            act = lax.convert_element_type(k, F32) < code
            buf[k] = jnp.where(act, star[k] + shift, 0.0)
            return carry

        lax.fori_loop(0, LEVELS, finish, 0, unroll=True)
        copies.append(pltpu.make_async_copy(buf, out, sem.at[4 + a]))
        copies[-1].start()
    for copy in copies:
        copy.wait()


def kernel(
    vel_u, vel_v, buoy, surface, trans_u, trans_v, ocean, layers,
    hbm_u, hbm_v, hbm_b, hbm_columns, hbm_wide,
    star_u, star_v, out_b, out_columns, out_wide, out_sem,
    fx, lp, dyb, near_ext, code_ext, in_3d, in_2d, in_int,
    x_send, y_send, x_recv, y_recv, gx_send, gy_send, gx_recv, gy_recv,
    fx_send, fy_send, fx_recv, fy_recv, in_sem, send_sem, recv_sem,
):
    loads = []
    for a, ref in enumerate((vel_u, vel_v, buoy)):
        loads.append(pltpu.make_async_copy(ref, in_3d.at[a], in_sem.at[a]))
    for a, ref in enumerate((surface, trans_u, trans_v)):
        loads.append(pltpu.make_async_copy(ref, in_2d.at[a], in_sem.at[3 + a]))
    for a, ref in enumerate((ocean, layers)):
        loads.append(pltpu.make_async_copy(ref, in_int.at[a], in_sem.at[6 + a]))
    for load in loads:
        load.start()
    gx, gy = lax.axis_index("gx"), lax.axis_index("gy")
    nx, ny = lax.axis_size("gx"), lax.axis_size("gy")

    def exists(d):
        ok = jnp.bool_(True)
        if d[0] == -1:
            ok = jnp.logical_and(ok, gx > 0)
        if d[0] == 1:
            ok = jnp.logical_and(ok, gx < nx - 1)
        if d[1] == -1:
            ok = jnp.logical_and(ok, gy > 0)
        if d[1] == 1:
            ok = jnp.logical_and(ok, gy < ny - 1)
        return ok

    here = {d: exists(d) for d in DIRS}
    barrier = pltpu.get_barrier_semaphore()
    total_near = jnp.int32(0)
    for d in DIRS:
        total_near = total_near + here[d].astype(jnp.int32)

        @pl.when(here[d])
        def _(d=d):
            pl.semaphore_signal(barrier, inc=1, device_id=(gx + d[0], gy + d[1]), device_id_type=MESH)

    for d in DIRS:
        @pl.when(jnp.logical_not(here[d]))
        def _(d=d):
            for p in range(STEPS):
                if d[1] == 0:
                    s = 0 if d[0] < 0 else 1
                    x_recv[p, s] = jnp.zeros(x_recv.shape[2:], F32)
                    gx_recv[p, s] = jnp.zeros(gx_recv.shape[2:], F32)
                    fx_recv[p, s] = jnp.zeros(fx_recv.shape[2:], F32)
                else:
                    s = SIDES.index(d)
                    y_recv[p, s] = jnp.zeros(y_recv.shape[2:], F32)
                    gy_recv[p, s] = jnp.zeros(gy_recv.shape[2:], F32)
                    fy_recv[p, s] = jnp.zeros(fy_recv.shape[2:], F32)

    def copies(phase, step):
        result = []
        for i, d in enumerate(DIRS):
            back = (-d[0], -d[1])
            if d[1] == 0:
                src_at, dst_at = (0 if d[0] < 0 else 1), (0 if back[0] < 0 else 1)
                if phase == FORCE:
                    src, dst = fx_send.at[step], fx_recv.at[step, dst_at]
                elif phase == PLANE:
                    rows = pl.ds(0, (4 if step == 0 else 3) * ROWS)
                    src, dst = gx_send.at[step, rows], gx_recv.at[step, dst_at, rows]
                else:
                    if step == 0:
                        rows = pl.ds(0, RIM)
                    elif phase == EARLY:
                        rows = pl.ds(2 * MOVING, 2 * LEVELS)
                    else:
                        rows = pl.ds(0, 2 * MOVING)
                    src, dst = x_send.at[step, src_at, rows], x_recv.at[step, dst_at, rows]
            else:
                src_at, dst_at = (0 if d[1] < 0 else 1), SIDES.index(back)
                if phase == FORCE:
                    src, dst = fy_send.at[step, src_at], fy_recv.at[step, dst_at]
                elif phase == PLANE:
                    src, dst = gy_send.at[step, src_at], gy_recv.at[step, dst_at]
                elif phase == EARLY:
                    continue
                else:
                    src, dst = y_send.at[step, src_at], y_recv.at[step, dst_at]
                    if d[0] != 0:
                        rows = pl.ds(0, 8) if d[0] < 0 else pl.ds(8, 8)
                        src, dst = src.at[rows], dst.at[rows]
            at = phase * STEPS + step
            copy = pltpu.make_async_remote_copy(
                src_ref=src, dst_ref=dst,
                send_sem=send_sem.at[at, i], recv_sem=recv_sem.at[at, DIRS.index(back)],
                device_id=(gx + d[0], gy + d[1]), device_id_type=MESH,
            )
            result.append((d, copy))
        return result

    def start(phase, step):
        for d, copy in copies(phase, step):
            @pl.when(here[d])
            def _(copy=copy):
                copy.start()

    def arrive(phase, step):
        by_dir = dict(copies(phase, step))
        for d in by_dir:
            @pl.when(here[d])
            def _(d=d):
                by_dir[(-d[0], -d[1])].wait_recv()

    def sent(phase, step):
        for d, copy in copies(phase, step):
            @pl.when(here[d])
            def _(copy=copy):
                copy.wait_send()

    lane = lax.broadcasted_iota(jnp.int32, (ROWS, LANES), 1)
    pair = lane >> 1
    odd = (lane & 1) == 1
    zero = jnp.zeros((ROWS, LANES), F32)

    def put(step, j, near_at, far_at, cells, strips):
        x_send[step, 0, pl.ds(near_at, 1)] = cells[0:1]
        x_send[step, 0, pl.ds(far_at, 1)] = cells[1:2]
        x_send[step, 1, pl.ds(near_at, 1)] = cells[ROWS - 1 : ROWS]
        x_send[step, 1, pl.ds(far_at, 1)] = cells[ROWS - 2 : ROWS - 1]
        to_left, to_right = strips
        rolled = turn(cells, 2 * j + 2, 1)
        to_right = jnp.where(pair == j, rolled, to_right)
        to_left = jnp.where(pair == j + 1, rolled, to_left)
        return to_left, to_right

    def put_v(step, j, cells, strips):
        fx[j, pl.ds(2, ROWS)] = cells
        return put(step, j, j, MOVING + j, cells, strips)

    def put_b(step, k, cells, strips):
        j = MOVING + k
        return put(step, j, 2 * MOVING + k, 2 * MOVING + LEVELS + k, cells, strips)

    def send_state(step, strips, flats):
        y_send[step, 0] = strips[0]
        y_send[step, 1] = strips[1]
        start(RIMS, step)
        flat_left, flat_right = pack_flat(flats)
        gy_send[step, 0] = flat_left
        gy_send[step, 1] = flat_right
        for a, cells in enumerate(flats):
            gx_send[step, ROWS * a : ROWS * (a + 1)] = cells
        start(PLANE, step)

    loads[6].wait()
    loads[7].wait()
    lay = in_int[1].astype(F32)
    code = jnp.where(in_int[0] > 0, lay, 0.0)
    strips = put(0, STACK, CODE_ROW, CODE_ROW + 1, code, (zero, zero))
    for a in range(FIELDS):
        loads[a].wait()

        def pack(k, strips, a=a):
            cells = in_3d[a, k]
            if a < 2:
                return put_v(0, a * LEVELS + k, cells, strips)
            fx[MOVING + k, pl.ds(2, ROWS)] = cells
            return put_b(0, k, cells, strips)

        strips = lax.fori_loop(0, LEVELS, pack, strips, unroll=True)
    for a in range(3):
        loads[3 + a].wait()
    pl.semaphore_wait(barrier, total_near)
    sea, flow_u, flow_v = in_2d[0], in_2d[1], in_2d[2]
    send_state(0, strips, (sea, flow_u, flow_v, code))

    lane18 = lax.broadcasted_iota(jnp.int32, (ROWS + 2, LANES), 1)
    for step in range(STEPS):
        arrive(RIMS, step)
        if step:
            arrive(EARLY, step)
        from_left, from_right = y_recv[step, 1], y_recv[step, 4]
        near = jnp.where(odd, from_left, turn(from_right, -2, 1))
        far = jnp.where(odd, turn(from_left, 1, 1), turn(from_right, -3, 1))
        inner = turn(jnp.where(odd, strips[1], strips[0]), -1, 1)
        near_ext[pl.ds(1, ROWS)] = near
        odd8 = odd[0:8]
        top = jnp.where(odd8, y_recv[step, 0, 8:16], turn(y_recv[step, 3, 8:16], -2, 1))
        low = jnp.where(odd8, y_recv[step, 2, 0:8], turn(y_recv[step, 5, 0:8], -2, 1))
        near_ext[pl.ds(0, 1)] = top[7:8]
        near_ext[pl.ds(ROWS + 1, 1)] = low[0:1]

        if step == 0:
            code_ext[pl.ds(0, 1)] = x_recv[0, 0, pl.ds(CODE_ROW, 1)]
            code_ext[pl.ds(1, ROWS)] = code
            code_ext[pl.ds(ROWS + 1, 1)] = x_recv[0, 1, pl.ds(CODE_ROW, 1)]
            at = 2 * STACK
            code_near = jnp.where(
                odd,
                jnp.broadcast_to(near[:, at + 1 : at + 2], (ROWS, LANES)),
                jnp.broadcast_to(near[:, at : at + 1], (ROWS, LANES)),
            )
            act_near = ((pair & (LEVELS - 1)).astype(F32) < code_near).astype(F32)
            code18 = code_ext[pl.ds(0, ROWS + 2)]
        lap_near = act_near * (
            far + inner + near_ext[pl.ds(0, ROWS)] + near_ext[pl.ds(2, ROWS)] - 4.0 * near
        )
        near18 = near_ext[pl.ds(0, ROWS + 2)]

        def biharm(j, near_at, far_at, act18, keep):
            fx[j, pl.ds(0, 1)] = x_recv[step, 0, pl.ds(far_at, 1)]
            fx[j, pl.ds(1, 1)] = x_recv[step, 0, pl.ds(near_at, 1)]
            fx[j, pl.ds(ROWS + 2, 1)] = x_recv[step, 1, pl.ds(near_at, 1)]
            fx[j, pl.ds(ROWS + 3, 1)] = x_recv[step, 1, pl.ds(far_at, 1)]
            mid = fx[j, pl.ds(1, ROWS + 2)]
            edge = turn(near18, 127 - 2 * j, 1)
            ahead = jnp.where(lane18 == LANES - 1, edge, turn(mid, -1, 1))
            behind = jnp.where(lane18 == 0, edge, turn(mid, 1, 1))
            lap = act18 * (
                fx[j, pl.ds(0, ROWS + 2)] + fx[j, pl.ds(2, ROWS + 2)] + ahead + behind - 4.0 * mid
            )
            lp[j, pl.ds(0, ROWS + 2)] = lap
            if keep is not None:
                dyb[keep, pl.ds(0, ROWS + 2)] = ahead - behind
            mid = lp[j, pl.ds(1, ROWS)]
            edge = turn(lap_near, 127 - 2 * j, 1)
            ahead = jnp.where(lane == LANES - 1, edge, turn(mid, -1, 1))
            behind = jnp.where(lane == 0, edge, turn(mid, 1, 1))
            return lp[j, pl.ds(0, ROWS)] + lp[j, pl.ds(2, ROWS)] + ahead + behind - 4.0 * mid

        def level(k, carry):
            press_x, press_y, force_u, force_v, col_u, col_v = carry
            level_at = lax.convert_element_type(k, F32)
            act18 = (level_at < code18).astype(F32)
            act = (level_at < code).astype(F32)
            bih_u = biharm(k, k, MOVING + k, act18, None)
            bih_v = biharm(LEVELS + k, LEVELS + k, MOVING + LEVELS + k, act18, None)
            bih_b = biharm(
                MOVING + k, 2 * MOVING + k, 2 * MOVING + LEVELS + k, act18, k
            )
            u, v = fx[k, pl.ds(2, ROWS)], fx[LEVELS + k, pl.ds(2, ROWS)]
            at = 2 * LEVELS + k
            b = fx[at, pl.ds(2, ROWS)]
            b_x = fx[at, pl.ds(3, ROWS)] - fx[at, pl.ds(1, ROWS)]
            b_y = dyb[k, pl.ds(1, ROWS)]
            press_x, press_y = press_x + b_x, press_y + b_y
            tend_u = (-0.25 / LEVELS) * press_x + 0.1 * v - 0.02 * bih_u
            tend_v = (-0.25 / LEVELS) * press_y - 0.1 * u - 0.02 * bih_v
            tend_b = -0.5 * (u * b_x + v * b_y) - 0.02 * bih_b
            su = act * (u + 0.2 * tend_u)
            sv = act * (v + 0.2 * tend_v)
            star_u[k] = su
            star_v[k] = sv
            new_b = act * (b + 0.2 * tend_b)
            if step == STEPS - 1:
                out_b[k] = new_b
            else:
                fx[at, pl.ds(2, ROWS)] = new_b
            return (
                press_x, press_y, force_u + act * tend_u, force_v + act * tend_v,
                col_u + su, col_v + sv,
            )

        _, _, force_u, force_v, col_u, col_v = lax.fori_loop(
            0, LEVELS, level, (zero,) * 6, unroll=True
        )
        force_u, force_v = force_u / LEVELS, force_v / LEVELS
        fx_send[step, 0:ROWS] = force_u
        fx_send[step, ROWS : 2 * ROWS] = force_v
        flat_left, flat_right = pack_flat((force_u, force_v))
        fy_send[step, 0] = flat_left
        fy_send[step, 1] = flat_right
        start(FORCE, step)
        if step == STEPS - 1:
            out_columns[0] = col_u
            out_columns[1] = col_v
            stores = [
                pltpu.make_async_copy(src, dst, out_sem.at[i])
                for i, (src, dst) in enumerate((
                    (star_u, hbm_u), (star_v, hbm_v), (out_b, hbm_b), (out_columns, hbm_columns),
                    (out_wide.at[0:4], hbm_wide.at[0:4]), (out_wide.at[4:6], hbm_wide.at[4:6]),
                ))
            ]
            for store in stores[:4]:
                store.start()

        if step < STEPS - 1:
            def pack_b(k, strips):
                return put_b(step + 1, k, fx[MOVING + k, pl.ds(2, ROWS)], strips)

            strips = lax.fori_loop(0, LEVELS, pack_b, (zero, zero), unroll=True)
            start(EARLY, step + 1)
        arrive(PLANE, step)
        sides = [gy_recv[step, r] for r in range(6)]

        def plane(own, a):
            rows = slice(ROWS * a, ROWS * (a + 1))
            return wide(own, gx_recv[step, 0, rows], gx_recv[step, 1, rows], sides, a)

        if step == 0:
            code_wide = plane(code, 3)
        state = (plane(sea, 0), plane(flow_u, 1), plane(flow_v, 2))
        if step == STEPS - 1:
            for a, cells in enumerate(state + (code_wide,)):
                out_wide[a] = cells
            stores[4].start()
        arrive(FORCE, step)
        sides_f = [fy_recv[step, r] for r in range(6)]
        push_u, push_v = (
            0.2 * wide(
                own, fx_recv[step, 0, ROWS * a : ROWS * (a + 1)],
                fx_recv[step, 1, ROWS * a : ROWS * (a + 1)], sides_f, a,
            )
            for a, own in enumerate((force_u, force_v))
        )
        if step == STEPS - 1:
            out_wide[4] = push_u
            out_wide[5] = push_v
            stores[5].start()
        else:
            (sea, flow_u, flow_v), sum_u, sum_v = barotropic(state, push_u, push_v, code_wide)
            scale = LEVELS / SUB
            shift_u = (scale * sum_u - col_u) / lay
            shift_v = (scale * sum_v - col_v) / lay

            def couple(k, strips):
                act = (lax.convert_element_type(k, F32) < code).astype(F32)
                strips = put_v(step + 1, k, act * (star_u[k] + shift_u), strips)
                return put_v(step + 1, LEVELS + k, act * (star_v[k] + shift_v), strips)

            strips = lax.fori_loop(0, LEVELS, couple, strips, unroll=True)
            send_state(step + 1, strips, (sea, flow_u, flow_v))

    for step in range(STEPS):
        for phase in (RIMS, FORCE, PLANE, EARLY):
            if phase != EARLY or step:
                sent(phase, step)
    for store in stores:
        store.wait()


def per_device(velocity_u, velocity_v, buoyancy, surface, transport_u, transport_v, ocean, layers):
    cube = jax.ShapeDtypeStruct(velocity_u.shape, F32)
    flat = jax.ShapeDtypeStruct(surface.shape, F32)
    hbm = pl.BlockSpec(memory_space=pltpu.HBM)
    ext = 24
    columns = jax.ShapeDtypeStruct((2, ROWS, LANES), F32)
    planes = jax.ShapeDtypeStruct((6, 3 * ROWS, 2 * LANES), F32)
    block = (LEVELS, ROWS, LANES)
    middle = pl.pallas_call(
        kernel,
        out_shape=(cube, cube, cube, columns, planes),
        in_specs=[hbm] * 8,
        out_specs=(hbm,) * 5,
        scratch_shapes=[
            pltpu.VMEM(block, F32),
            pltpu.VMEM(block, F32),
            pltpu.VMEM(block, F32),
            pltpu.VMEM(columns.shape, F32),
            pltpu.VMEM(planes.shape, F32),
            pltpu.SemaphoreType.DMA((6,)),
            pltpu.VMEM((STACK, ext, LANES), F32),
            pltpu.VMEM((STACK, ext, LANES), F32),
            pltpu.VMEM((LEVELS, ext, LANES), F32),
            pltpu.VMEM((ext, LANES), F32),
            pltpu.VMEM((ext, LANES), F32),
            pltpu.VMEM((FIELDS,) + block, F32),
            pltpu.VMEM((3, ROWS, LANES), F32),
            pltpu.VMEM((2, ROWS, LANES), jnp.int32),
            pltpu.VMEM((STEPS, 2, RIM, LANES), F32),
            pltpu.VMEM((STEPS, 2, ROWS, LANES), F32),
            pltpu.VMEM((STEPS, 2, RIM, LANES), F32),
            pltpu.VMEM((STEPS, 6, ROWS, LANES), F32),
            pltpu.VMEM((STEPS, 4 * ROWS, LANES), F32),
            pltpu.VMEM((STEPS, 2, 8, LANES), F32),
            pltpu.VMEM((STEPS, 2, 4 * ROWS, LANES), F32),
            pltpu.VMEM((STEPS, 6, 8, LANES), F32),
            pltpu.VMEM((STEPS, 2 * ROWS, LANES), F32),
            pltpu.VMEM((STEPS, 2, 8, LANES), F32),
            pltpu.VMEM((STEPS, 2, 2 * ROWS, LANES), F32),
            pltpu.VMEM((STEPS, 6, 8, LANES), F32),
            pltpu.SemaphoreType.DMA((8,)),
            pltpu.SemaphoreType.DMA((4 * STEPS, 8)),
            pltpu.SemaphoreType.DMA((4 * STEPS, 8)),
        ],
        compiler_params=pltpu.CompilerParams(
            collective_id=0, has_side_effects=True, vmem_limit_bytes=60 * 2**20
        ),
    )(velocity_u, velocity_v, buoyancy, surface, transport_u, transport_v, ocean, layers)
    return tuple(
        pl.pallas_call(
            finish_kernel,
            out_shape=(cube, cube, cube, flat, flat, flat),
            in_specs=[hbm] * 5,
            out_specs=(hbm,) * 6,
            scratch_shapes=[
                pltpu.VMEM(block, F32),
                pltpu.VMEM(block, F32),
                pltpu.VMEM(columns.shape, F32),
                pltpu.VMEM(planes.shape, F32),
                pltpu.VMEM(block, F32),
                pltpu.VMEM(block, F32),
                pltpu.VMEM((3, ROWS, LANES), F32),
                pltpu.SemaphoreType.DMA((6,)),
                pltpu.SemaphoreType.DMA((4,)),
            ],
            compiler_params=pltpu.CompilerParams(vmem_limit_bytes=60 * 2**20),
        )(*middle)
    )


def solution(mesh):
    cube, flat = P(None, "gx", "gy"), P("gx", "gy")
    return jax.shard_map(
        per_device,
        mesh=mesh,
        in_specs=(cube, cube, cube, flat, flat, flat, flat, flat),
        out_specs=(cube, cube, cube, flat, flat, flat),
        check_vma=False,
    )
```

time: 46.3 us -> 36.4 us (0.79)
  local copies, waits for them, and re-layouts: 9.95 us -> 0 us
    unnamed x22 -> x0, local copies, waits for them, and re-layouts: 9.95 us -> none
    pallas_call x1 -> x2, Pallas kernels: 35.3 us -> 35.5 us  [the longest x1 30.4 us: per_device(): pl.pallas_call(kernel, out_shape=(cube, cube, cube, columns, planes), in_...]
where the time goes in v2:
time: 36.4 us; the launch traced here: 36.2 us
  Pallas kernels  35.5 us (98%)
  between operations  0.64 us (2%)
    pallas_call x1, Pallas kernels, per_device(): pl.pallas_call(kernel, out_shape=(cube, cube, cube, columns, planes), in_...  30.4 us
    pallas_call x1, Pallas kernels, per_device(): pl.pallas_call(finish_kernel, out_shape=(cube, cube, cube, flat, flat, fl...  5.18 us

profile of v2, /device:TPU:1, one launch (start us, length us, event | category | flops | bytes accessed | tf_op | source)
XLA Modules:
  0.0 36.2 jit_solution(9530154817274198330)
XLA Ops:
  0.6 30.4 %shard_map.127 = (f32[16,16,128]{2,1,0:T(8,128)}, f32[16,16,128]{2,1,0:T(8,128)}, f32[16,16,128]{2,1,0:T(8,128)}, f32[2,16,128]{2,1,0:T(8,128)}, f32[6,48,256]{2,1,0:T(8,128)}) custom-call(f32[16,16,128]{2,1,0:T(8,128)} %vel_u.1, f32[16,16,128]{2,1,0:T(8,128)} %vel_v.1, f32[16,16,128]{2,1,0:T(8,128)} %buoy.1, f32[16,128]{1,0:T(8,128)} %surface.1, ...), custom_call_target="tpu_custom_call" | custom-call | tf_op jit(solution)/shard_map/pallas_call | solution.py:480
  31.0 5.2 %shard_map.128 = (f32[16,16,128]{2,1,0:T(8,128)}, f32[16,16,128]{2,1,0:T(8,128)}, f32[16,16,128]{2,1,0:T(8,128)}, f32[16,128]{1,0:T(8,128)}, f32[16,128]{1,0:T(8,128)}, /*index=5*/f32[16,128]{1,0:T(8,128)}) custom-call(f32[16,16,128]{2,1,0:T(8,128)} %get-tuple-element.11.hbm_u, f32[16,16,128]{2,1,0:T(8,128)} %get-tuple-element.12.hbm_v, ...), custom_call_target="tpu_custom_call" | custom-call | tf_op jit(solution)/shard_map/pallas_call | solution.py:521

commit v3 on v2

--- a/solution.py
+++ b/solution.py
@@ -79,7 +79,9 @@
         sum_v = sum_v + new_v[ROWS : 2 * ROWS, 0:LANES]
         return eta, new_u, new_v, sum_u, sum_v
 
-    eta, tu, tv, sum_u, sum_v = lax.fori_loop(0, SUB, substep, state + (zero, zero))
+    eta, tu, tv, sum_u, sum_v = lax.fori_loop(
+        0, SUB, substep, state + (zero, zero), unroll=True
+    )
     own = tuple(c[ROWS : 2 * ROWS, 0:LANES] for c in (eta, tu, tv))
     return own, sum_u, sum_v
 
@@ -337,7 +339,7 @@
         )
         near18 = near_ext[pl.ds(0, ROWS + 2)]
 
-        def biharm(j, near_at, far_at, act18, keep):
+        def biharm(j, near_at, far_at, act18):
             fx[j, pl.ds(0, 1)] = x_recv[step, 0, pl.ds(far_at, 1)]
             fx[j, pl.ds(1, 1)] = x_recv[step, 0, pl.ds(near_at, 1)]
             fx[j, pl.ds(ROWS + 2, 1)] = x_recv[step, 1, pl.ds(near_at, 1)]
@@ -350,42 +352,54 @@
                 fx[j, pl.ds(0, ROWS + 2)] + fx[j, pl.ds(2, ROWS + 2)] + ahead + behind - 4.0 * mid
             )
             lp[j, pl.ds(0, ROWS + 2)] = lap
-            if keep is not None:
-                dyb[keep, pl.ds(0, ROWS + 2)] = ahead - behind
             mid = lp[j, pl.ds(1, ROWS)]
             edge = turn(lap_near, 127 - 2 * j, 1)
             ahead = jnp.where(lane == LANES - 1, edge, turn(mid, -1, 1))
             behind = jnp.where(lane == 0, edge, turn(mid, 1, 1))
             return lp[j, pl.ds(0, ROWS)] + lp[j, pl.ds(2, ROWS)] + ahead + behind - 4.0 * mid
 
+        def buoyancy(k, carry):
+            level_at = lax.convert_element_type(k, F32)
+            act18 = (level_at < code18).astype(F32)
+            act = (level_at < code).astype(F32)
+            at = 2 * LEVELS + k
+            bih_b = biharm(at, 2 * MOVING + k, 2 * MOVING + LEVELS + k, act18)
+            u, v = fx[k, pl.ds(2, ROWS)], fx[LEVELS + k, pl.ds(2, ROWS)]
+            b = fx[at, pl.ds(2, ROWS)]
+            b_x = fx[at, pl.ds(3, ROWS)] - fx[at, pl.ds(1, ROWS)]
+            tend_b = -0.5 * (u * b_x + v * dyb[k, pl.ds(0, ROWS)]) - 0.02 * bih_b
+            new_b = act * (b + 0.2 * tend_b)
+            if step == STEPS - 1:
+                out_b[k] = new_b
+            else:
+                fx[at, pl.ds(2, ROWS)] = new_b
+            return carry
+
         def level(k, carry):
             press_x, press_y, force_u, force_v, col_u, col_v = carry
             level_at = lax.convert_element_type(k, F32)
             act18 = (level_at < code18).astype(F32)
             act = (level_at < code).astype(F32)
-            bih_u = biharm(k, k, MOVING + k, act18, None)
-            bih_v = biharm(LEVELS + k, LEVELS + k, MOVING + LEVELS + k, act18, None)
-            bih_b = biharm(
-                MOVING + k, 2 * MOVING + k, 2 * MOVING + LEVELS + k, act18, k
-            )
+            bih_u = biharm(k, k, MOVING + k, act18)
+            bih_v = biharm(LEVELS + k, LEVELS + k, MOVING + LEVELS + k, act18)
             u, v = fx[k, pl.ds(2, ROWS)], fx[LEVELS + k, pl.ds(2, ROWS)]
             at = 2 * LEVELS + k
+            fx[at, pl.ds(1, 1)] = x_recv[step, 0, pl.ds(2 * MOVING + k, 1)]
+            fx[at, pl.ds(ROWS + 2, 1)] = x_recv[step, 1, pl.ds(2 * MOVING + k, 1)]
             b = fx[at, pl.ds(2, ROWS)]
+            edge = turn(near, 127 - 2 * at, 1)
             b_x = fx[at, pl.ds(3, ROWS)] - fx[at, pl.ds(1, ROWS)]
-            b_y = dyb[k, pl.ds(1, ROWS)]
+            b_y = jnp.where(lane == LANES - 1, edge, turn(b, -1, 1)) - jnp.where(
+                lane == 0, edge, turn(b, 1, 1)
+            )
+            dyb[k, pl.ds(0, ROWS)] = b_y
             press_x, press_y = press_x + b_x, press_y + b_y
             tend_u = (-0.25 / LEVELS) * press_x + 0.1 * v - 0.02 * bih_u
             tend_v = (-0.25 / LEVELS) * press_y - 0.1 * u - 0.02 * bih_v
-            tend_b = -0.5 * (u * b_x + v * b_y) - 0.02 * bih_b
             su = act * (u + 0.2 * tend_u)
             sv = act * (v + 0.2 * tend_v)
             star_u[k] = su
             star_v[k] = sv
-            new_b = act * (b + 0.2 * tend_b)
-            if step == STEPS - 1:
-                out_b[k] = new_b
-            else:
-                fx[at, pl.ds(2, ROWS)] = new_b
             return (
                 press_x, press_y, force_u + act * tend_u, force_v + act * tend_v,
                 col_u + su, col_v + sv,
@@ -401,6 +415,7 @@
         fy_send[step, 0] = flat_left
         fy_send[step, 1] = flat_right
         start(FORCE, step)
+        lax.fori_loop(0, LEVELS, buoyancy, 0, unroll=True)
         if step == STEPS - 1:
             out_columns[0] = col_u
             out_columns[1] = col_v

time: 36.4 us -> 35.5 us (0.975)
  Pallas kernels: 35.5 us -> 34.6 us
    pallas_call x1, Pallas kernels: 30.4 us -> 29.5 us  [per_device(): pl.pallas_call(kernel, out_shape=(cube, cube, cube, columns, planes), in_...]
where the time goes in v3:
time: 35.5 us; the launch traced here: 35.3 us
  Pallas kernels  34.6 us (97%)
  between operations  0.64 us (2%)
    pallas_call x1, Pallas kernels, per_device(): pl.pallas_call(kernel, out_shape=(cube, cube, cube, columns, planes), in_...  29.5 us
    pallas_call x1, Pallas kernels, per_device(): pl.pallas_call(finish_kernel, out_shape=(cube, cube, cube, flat, flat, fl...  5.18 us

profile of v3, /device:TPU:1, one launch (start us, length us, event | category | flops | bytes accessed | tf_op | source)
XLA Modules:
  0.0 35.3 jit_solution(12392314101511646699)
XLA Ops:
  0.6 29.5 %shard_map.127 = (f32[16,16,128]{2,1,0:T(8,128)}, f32[16,16,128]{2,1,0:T(8,128)}, f32[16,16,128]{2,1,0:T(8,128)}, f32[2,16,128]{2,1,0:T(8,128)}, f32[6,48,256]{2,1,0:T(8,128)}) custom-call(f32[16,16,128]{2,1,0:T(8,128)} %vel_u.1, f32[16,16,128]{2,1,0:T(8,128)} %vel_v.1, f32[16,16,128]{2,1,0:T(8,128)} %buoy.1, f32[16,128]{1,0:T(8,128)} %surface.1, ...), custom_call_target="tpu_custom_call" | custom-call | tf_op jit(solution)/shard_map/pallas_call | solution.py:495
  30.1 5.2 %shard_map.128 = (f32[16,16,128]{2,1,0:T(8,128)}, f32[16,16,128]{2,1,0:T(8,128)}, f32[16,16,128]{2,1,0:T(8,128)}, f32[16,128]{1,0:T(8,128)}, f32[16,128]{1,0:T(8,128)}, /*index=5*/f32[16,128]{1,0:T(8,128)}) custom-call(f32[16,16,128]{2,1,0:T(8,128)} %get-tuple-element.11.hbm_u, f32[16,16,128]{2,1,0:T(8,128)} %get-tuple-element.12.hbm_v, ...), custom_call_target="tpu_custom_call" | custom-call | tf_op jit(solution)/shard_map/pallas_call | solution.py:536
